TPU v7x, 256 devices: a whole 4x4x8 slice. The times are simulated.
256 devices in a mesh: gx: 4 (over x), gy: 8 (over z), gz: 8 (over y, core).
Axes of the slice: x: 4, y: 4, z: 8, core: 2. Of those that a mesh axis runs over, the one named last changes fastest.
Arguments:
- right_side: float32 [64, 256, 1024], P('gx', 'gy', 'gz'), may hold values from -4 to 4
- coefficient: float32 [64, 256, 1024], P('gx', 'gy', 'gz'), may hold values from 0.25 to 4
- guess: float32 [64, 256, 1024], P('gx', 'gy', 'gz'), may hold values from -6 to 6
Outputs:
- iterate: float32 [64, 256, 1024], P('gx', 'gy', 'gz')
All inputs are finite; a program needn't handle non-finite values.
Results may differ from a plain program's by a relative error of at most 0.0001.
Values sent between devices are 32-bit elements; how exact they have to be, the bound alone decides.
A program may use at most 128 MiB of HBM per device.

v0:
```python
import jax
import jax.numpy as jnp
from jax import lax
from jax.sharding import PartitionSpec as P

SWEEPS = 2
CHEB = 20


OMEGA = 2.0 / 3.0
CHEB_LOW = 0.1
CHEB_HIGH = 2.0
OFFSETS = ((2, 1, 1), (0, 1, 1), (1, 2, 1), (1, 0, 1), (1, 1, 2), (1, 1, 0))


def extended(shard, sides, width):
    for axis, dim in sides:
        size, length = (lax.axis_size(axis), shard.shape[dim])
        up = [(i, (i + 1) % size) for i in range(size - 1)]
        down = [(j, i) for i, j in up]
        last = lax.slice_in_dim(shard, length - width, length, axis=dim)
        leading = lax.slice_in_dim(shard, 0, width, axis=dim)
        before = lax.ppermute(last, axis, up)
        after = lax.ppermute(leading, axis, down)
        shard = jnp.concatenate([before, shard, after], axis=dim)
    return shard


def restrict(field):
    size_x, size_y, size_z = field.shape
    return field.reshape(size_x // 2, 2, size_y // 2, 2, size_z // 2, 2).mean(axis=(1, 3, 5))


def prolong(field):
    return jnp.repeat(jnp.repeat(jnp.repeat(field, 2, axis=0), 2, axis=1), 2, axis=2)


def neighbour(padded, offset):
    return padded[
        offset[0] : offset[0] + padded.shape[0] - 2,
        offset[1] : offset[1] + padded.shape[1] - 2,
        offset[2] : offset[2] + padded.shape[2] - 2,
    ]


def diagonal(padded_coef, scale):
    centre = padded_coef[1:-1, 1:-1, 1:-1]
    total = jnp.zeros_like(centre)
    for offset in OFFSETS:
        total = total + 0.5 * (centre + neighbour(padded_coef, offset))
    return scale * total


def operate(padded_field, padded_coef, scale):
    centre = padded_coef[1:-1, 1:-1, 1:-1]
    value = padded_field[1:-1, 1:-1, 1:-1]
    total = jnp.zeros_like(value)
    for offset in OFFSETS:
        total = total + 0.5 * (centre + neighbour(padded_coef, offset)) * (
            value - neighbour(padded_field, offset)
        )
    return scale * total


def fine_halo(field):
    return extended(field, (("gx", 0), ("gy", 1), ("gz", 2)), 1)


def mid_halo(field):
    return extended(field, (("gx", 0), ("gy", 1), ("gz", 2)), 1)


def smooth_once(field, target, padded_coef, diag, scale, halo_fn):
    return field + OMEGA * (target - operate(halo_fn(field), padded_coef, scale)) / diag


def chebyshev(target, coef, scale):
    padded_coef = jnp.pad(coef, 1)
    diag = diagonal(padded_coef, scale)
    theta = 0.5 * (CHEB_HIGH + CHEB_LOW)
    delta = 0.5 * (CHEB_HIGH - CHEB_LOW)
    sigma = theta / delta
    step = target / diag / theta
    rho = jnp.float32(1.0 / sigma)

    def update(count, carry):
        solution, step, rho = carry
        resid = target - operate(jnp.pad(solution, 1), padded_coef, scale)
        rho_next = 1.0 / (2.0 * sigma - rho)
        step = rho_next * rho * step + 2.0 * rho_next / delta * resid / diag
        return (solution + step, step, rho_next)

    solution, step, rho = lax.fori_loop(0, CHEB - 1, update, (step, step, rho))
    return solution


def unpack(stack, count_x, count_y, count_z):
    parts, size_x, size_y, size_z = stack.shape
    grid = stack.reshape(count_x, count_y, count_z, size_x, size_y, size_z)
    return grid.transpose(0, 3, 1, 4, 2, 5).reshape(
        count_x * size_x, count_y * size_y, count_z * size_z
    )


def on_device(right_side, coefficient, guess):
    scales = (1.0, 0.25, 0.0625, 0.015625)
    index_x = lax.axis_index("gx")
    index_y = lax.axis_index("gy")
    index_z = lax.axis_index("gz")
    coef_one = restrict(coefficient)
    coef_two = restrict(coef_one)
    padded_fine = fine_halo(coefficient)
    padded_one = None
    diag_fine = diagonal(padded_fine, scales[0])
    field = guess
    for sweep in range(SWEEPS):
        field = smooth_once(field, right_side, padded_fine, diag_fine, scales[0], fine_halo)
    target_one = restrict(right_side - operate(fine_halo(field), padded_fine, scales[0]))
    padded_one = mid_halo(coef_one)
    diag_one = diagonal(padded_one, scales[1])
    error_one = OMEGA * target_one / diag_one
    error_one = smooth_once(error_one, target_one, padded_one, diag_one, scales[1], mid_halo)
    target_two = restrict(target_one - operate(mid_halo(error_one), padded_one, scales[1]))
    padded_two = mid_halo(coef_two)
    diag_two = diagonal(padded_two, scales[2])
    error_two = OMEGA * target_two / diag_two
    error_two = smooth_once(error_two, target_two, padded_two, diag_two, scales[2], mid_halo)
    resid_two = target_two - operate(mid_halo(error_two), padded_two, scales[2])
    target_three = restrict(resid_two)
    coef_three = restrict(coef_two)
    small_x, small_y, small_z = target_three.shape
    stacks = (
        lax.all_gather(target_three[None], ("gx", "gy", "gz"), axis=0, tiled=True),
        lax.all_gather(coef_three[None], ("gx", "gy", "gz"), axis=0, tiled=True),
    )
    count_x, count_y, count_z = (lax.axis_size("gx"), lax.axis_size("gy"), lax.axis_size("gz"))
    all_target = unpack(stacks[0], count_x, count_y, count_z)
    all_coef = unpack(stacks[1], count_x, count_y, count_z)
    coarse = chebyshev(all_target, all_coef, scales[3])
    starts = (index_x * small_x, index_y * small_y, index_z * small_z)
    region = lax.dynamic_slice(coarse, starts, (small_x, small_y, small_z))
    error_two = error_two + prolong(region)
    for sweep in range(SWEEPS):
        error_two = smooth_once(error_two, target_two, padded_two, diag_two, scales[2], mid_halo)
    error_one = error_one + prolong(error_two)
    for sweep in range(SWEEPS):
        error_one = smooth_once(error_one, target_one, padded_one, diag_one, scales[1], mid_halo)
    field = field + prolong(error_one)
    for sweep in range(SWEEPS):
        field = smooth_once(field, right_side, padded_fine, diag_fine, scales[0], fine_halo)
    return field


def solution(mesh):
    in_specs = (P("gx", "gy", "gz"), P("gx", "gy", "gz"), P("gx", "gy", "gz"))
    out_specs = P("gx", "gy", "gz")
    return jax.shard_map(
        on_device, mesh=mesh, in_specs=in_specs, out_specs=out_specs, check_vma=False
    )
```

profile of v0, /device:TPU:1, one launch (start us, length us, event | category | flops | bytes accessed | tf_op | source)
XLA Modules:
  0.0 579.6 jit_solution(9985866857225409384)
XLA Ops:
  8.0 4.7 collective-permute-start.2
  12.8 18.9 %reshape.78 = f32[8,2,16,2,64,2]{5,4,3,2,1,0:T(8,128)} reshape(f32[16,32,128]{2,1,0:T(8,128)} %param.6) | data formatting | bytes 524288 | tf_op jit(solution)/shard_map/reshape | solution.py:31
  31.7 7.0 %reduce_sum.55 = f32[8,16,64]{2,1,0:T(8,128)S(1)} reduce(f32[8,2,16,2,64,2]{5,4,3,2,1,0:T(8,128)} %reshape.78, f32[]{:T(128)} %constant.89.clone.1), dimensions={1,3,5}, to_apply=%region_1.0 | reduce | flops 57344 | bytes 294916 | tf_op jit(solution)/shard_map/reduce_sum | solution.py:31
  51.0 5.3 collective-permute-start.11
  96.3 4.8 collective-permute-start.17
  118.2 5.2 collective-permute-start.27
  124.7 5.5 collective-permute-start.21
  143.7 18.1 %reshape.77 = f32[8,2,16,2,64,2]{5,4,3,2,1,0:T(8,128)} reshape(f32[16,32,128]{2,1,0:T(8,128)S(1)} %fusion.67) | data formatting | bytes 524288 | tf_op jit(solution)/shard_map/reshape | solution.py:31
  161.8 7.0 %reduce_sum.54 = f32[8,16,64]{2,1,0:T(8,128)S(1)} reduce(f32[8,2,16,2,64,2]{5,4,3,2,1,0:T(8,128)} %reshape.77, f32[]{:T(128)} %constant.89.clone.1), dimensions={1,3,5}, to_apply=%region_0.0 | reduce | flops 57344 | bytes 294916 | tf_op jit(solution)/shard_map/reduce_sum | solution.py:31
  175.9 5.5 collective-permute-start.45
  182.7 5.5 collective-permute-start.33
  206.6 5.5 collective-permute-start.39
  233.9 4.5 collective-permute-start.49
  239.2 5.1 collective-permute-start.51
  244.3 68.0 %all-gather.1 = f32[512,4,16]{2,1,0:T(4,128)S(1)} all-gather(f32[2,4,16]{2,1,0:T(4,128)S(1)} %broadcast_multiply_fusion.2), channel_id=3, replica_groups=mesh['gx'=4,'gy'=8,'gz'=8] {'gx','gy','gz'}, dimensions={0}, use_global_device_ids=true | all-gather | bytes 131584 | tf_op jit(solution)/shard_map/all_gather | solution.py:134
  326.5 4.6 collective-permute-start.55
  353.0 63.3 %all-gather = f32[512,4,16]{2,1,0:T(4,128)S(1)} all-gather(f32[2,4,16]{2,1,0:T(4,128)S(1)} %broadcast_multiply_fusion.3), channel_id=2, replica_groups=mesh['gx'=4,'gy'=8,'gz'=8] {'gx','gy','gz'}, dimensions={0}, use_global_device_ids=true | all-gather | bytes 131584 | tf_op jit(solution)/shard_map/all_gather | solution.py:133
  417.1 5.7 while.16
  479.1 4.7 collective-permute-start.75
  484.6 5.9 %collective-permute-start.77 = (f32[10,18,1]{2,1,0:T(8,128)S(1)}, f32[10,18,1]{2,1,0:T(8,128)S(1)}, u32[]{:S(2)}, u32[]{:S(2)}) collective-permute-start(f32[10,18,1]{2,1,0:T(8,128)S(1)} %get-tuple-element.209), channel_id=1, source_target_pairs={{0,1},{1,2},{2,3},{3,4},{4,5},{5,6},{6,7},{8,9},{9,10},{10,11},{11... | collective-permute-start | bytes 2168 | tf_op jit(solution)/shard_map/ppermute | solution.py:23
  499.1 4.5 collective-permute-start.79
  526.0 4.5 collective-permute-start.85
  553.1 4.5 collective-permute-start.91
  559.9 4.5 collective-permute-start.93
  (437 shorter events, 308.6 us)
Async XLA Ops:
  0.7 38.0 %collective-permute-start.3 = (f32[1,32,128]{2,1,0:T(8,128)S(1)}, f32[1,32,128]{2,1,0:T(8,128)S(1)}, u32[]{:S(2)}, u32[]{:S(2)}) collective-permute-start(f32[1,32,128]{2,1,0:T(8,128)S(1)} %get-tuple-element.205), channel_id=1, source_target_pairs={{0,64},{64,128},{128,192},{1,65},{65,129},{129,193},{2,66},{66,130... | collective-permute-start | bytes 49160 | tf_op jit(solution)/shard_map/ppermute | solution.py:23
  4.7 34.1 %collective-permute-start.1 = (f32[1,32,128]{2,1,0:T(8,128)S(1)}, f32[1,32,128]{2,1,0:T(8,128)S(1)}, u32[]{:S(2)}, u32[]{:S(2)}) collective-permute-start(f32[1,32,128]{2,1,0:T(8,128)S(1)} %get-tuple-element.204), channel_id=1, source_target_pairs={{64,0},{128,64},{192,128},{65,1},{129,65},{193,129},{66,2},{130,66... | collective-permute-start | bytes 49160 | tf_op jit(solution)/shard_map/ppermute | solution.py:24
  6.7 37.6 %collective-permute-start = (f32[1,32,128]{2,1,0:T(8,128)S(1)}, f32[1,32,128]{2,1,0:T(8,128)S(1)}, u32[]{:S(2)}, u32[]{:S(2)}) collective-permute-start(f32[1,32,128]{2,1,0:T(8,128)S(1)} %get-tuple-element.203), channel_id=1, source_target_pairs={{64,0},{128,64},{192,128},{65,1},{129,65},{193,129},{66,2},{130,66... | collective-permute-start | bytes 49160 | tf_op jit(solution)/shard_map/ppermute | solution.py:24
  8.0 36.3 %collective-permute-start.2 = (f32[1,32,128]{2,1,0:T(8,128)S(1)}, f32[1,32,128]{2,1,0:T(8,128)S(1)}, u32[]{:S(2)}, u32[]{:S(2)}) collective-permute-start(f32[1,32,128]{2,1,0:T(8,128)S(1)} %get-tuple-element.202), channel_id=1, source_target_pairs={{0,64},{64,128},{128,192},{1,65},{65,129},{129,193},{2,66},{66,130... | collective-permute-start | bytes 49160 | tf_op jit(solution)/shard_map/ppermute | solution.py:23
  44.4 13.8 %collective-permute-start.4 = (f32[18,1,128]{2,1,0:T(1,128)S(1)}, f32[18,1,128]{2,1,0:T(1,128)S(1)}, u32[]{:S(2)}, u32[]{:S(2)}) collective-permute-start(f32[18,1,128]{2,1,0:T(1,128)S(1)} %get-tuple-element.191), channel_id=1, source_target_pairs={{8,0},{16,8},{24,16},{32,24},{40,32},{48,40},{56,48},{9,1},{17,9},... | collective-permute-start | bytes 27656 | tf_op jit(solution)/shard_map/ppermute | solution.py:24
  45.7 12.6 %collective-permute-start.6 = (f32[18,1,128]{2,1,0:T(1,128)S(1)}, f32[18,1,128]{2,1,0:T(1,128)S(1)}, u32[]{:S(2)}, u32[]{:S(2)}) collective-permute-start(f32[18,1,128]{2,1,0:T(1,128)S(1)} %get-tuple-element.190), channel_id=1, source_target_pairs={{0,8},{8,16},{16,24},{24,32},{32,40},{40,48},{48,56},{1,9},{9,17},... | collective-permute-start | bytes 27656 | tf_op jit(solution)/shard_map/ppermute | solution.py:23
  51.0 18.8 %collective-permute-start.11 = (f32[18,34,1]{2,1,0:T(8,128)}, f32[18,34,1]{2,1,0:T(8,128)}, u32[]{:S(2)}, u32[]{:S(2)}) collective-permute-start(f32[18,34,1]{2,1,0:T(8,128)} %get-tuple-element.181), channel_id=1, source_target_pairs={{0,1},{1,2},{2,3},{3,4},{4,5},{5,6},{6,7},{8,9},{9,10},{10,11},{11... | collective-permute-start | bytes 7352 | tf_op jit(solution)/shard_map/ppermute | solution.py:23
  56.3 17.7 %collective-permute-start.9 = (f32[18,34,1]{2,1,0:T(8,128)}, f32[18,34,1]{2,1,0:T(8,128)}, u32[]{:S(2)}, u32[]{:S(2)}) collective-permute-start(f32[18,34,1]{2,1,0:T(8,128)} %get-tuple-element.180), channel_id=1, source_target_pairs={{1,0},{2,1},{3,2},{4,3},{5,4},{6,5},{7,6},{9,8},{10,9},{11,10},{12... | collective-permute-start | bytes 7352 | tf_op jit(solution)/shard_map/ppermute | solution.py:24
  59.4 14.7 %collective-permute-start.8 = (f32[18,34,1]{2,1,0:T(8,128)}, f32[18,34,1]{2,1,0:T(8,128)S(1)}, u32[]{:S(2)}, u32[]{:S(2)}) collective-permute-start(f32[18,34,1]{2,1,0:T(8,128)} %get-tuple-element.179), channel_id=1, source_target_pairs={{1,0},{2,1},{3,2},{4,3},{5,4},{6,5},{7,6},{9,8},{10,9},{11,10},{12... | collective-permute-start | bytes 7352 | tf_op jit(solution)/shard_map/ppermute | solution.py:24
  61.3 13.6 %collective-permute-start.10 = (f32[18,34,1]{2,1,0:T(8,128)}, f32[18,34,1]{2,1,0:T(8,128)}, u32[]{:S(2)}, u32[]{:S(2)}) collective-permute-start(f32[18,34,1]{2,1,0:T(8,128)} %get-tuple-element.178), channel_id=1, source_target_pairs={{0,1},{1,2},{2,3},{3,4},{4,5},{5,6},{6,7},{8,9},{9,10},{10,11},{11... | collective-permute-start | bytes 7352 | tf_op jit(solution)/shard_map/ppermute | solution.py:23
  65.6 51.2 %collective-permute-start.24 = (f32[1,16,64]{2,1,0:T(8,128)}, f32[1,16,64]{2,1,0:T(8,128)S(1)}, u32[]{:S(2)}, u32[]{:S(2)}) collective-permute-start(f32[1,16,64]{2,1,0:T(8,128)} %get-tuple-element.235), channel_id=1, source_target_pairs={{64,0},{128,64},{192,128},{65,1},{129,65},{193,129},{66,2},{130,66... | collective-permute-start | bytes 12296 | tf_op jit(solution)/shard_map/ppermute | solution.py:24
  69.8 47.0 %collective-permute-start.25 = (f32[1,16,64]{2,1,0:T(8,128)}, f32[1,16,64]{2,1,0:T(8,128)S(1)}, u32[]{:S(2)}, u32[]{:S(2)}) collective-permute-start(f32[1,16,64]{2,1,0:T(8,128)} %get-tuple-element.234), channel_id=1, source_target_pairs={{0,64},{64,128},{128,192},{1,65},{65,129},{129,193},{2,66},{66,130... | collective-permute-start | bytes 12296 | tf_op jit(solution)/shard_map/ppermute | solution.py:23
  89.6 11.4 %collective-permute-start.42 = (f32[1,8,32]{2,1,0:T(8,128)S(1)}, f32[1,8,32]{2,1,0:T(8,128)S(1)}, u32[]{:S(2)}, u32[]{:S(2)}) collective-permute-start(f32[1,8,32]{2,1,0:T(8,128)S(1)} %get-tuple-element.275), channel_id=1, source_target_pairs={{64,0},{128,64},{192,128},{65,1},{129,65},{193,129},{66,2},{130,66... | collective-permute-start | bytes 3080 | tf_op jit(solution)/shard_map/ppermute | solution.py:24
  111.2 12.2 %collective-permute-start.18 = (f32[1,32,128]{2,1,0:T(8,128)S(1)}, f32[1,32,128]{2,1,0:T(8,128)S(1)}, u32[]{:S(2)}, u32[]{:S(2)}) collective-permute-start(f32[1,32,128]{2,1,0:T(8,128)S(1)} %get-tuple-element.199), channel_id=1, source_target_pairs={{64,0},{128,64},{192,128},{65,1},{129,65},{193,129},{66,2},{130,66... | collective-permute-start | bytes 49160 | tf_op jit(solution)/shard_map/ppermute | solution.py:24
  116.9 13.3 %collective-permute-start.26 = (f32[10,1,64]{2,1,0:T(1,128)S(1)}, f32[10,1,64]{2,1,0:T(1,128)S(1)}, u32[]{:S(2)}, u32[]{:S(2)}) collective-permute-start(f32[10,1,64]{2,1,0:T(1,128)S(1)} %get-tuple-element.225), channel_id=1, source_target_pairs={{8,0},{16,8},{24,16},{32,24},{40,32},{48,40},{56,48},{9,1},{17,9},... | collective-permute-start | bytes 7688 | tf_op jit(solution)/shard_map/ppermute | solution.py:24
  118.2 12.1 %collective-permute-start.27 = (f32[10,1,64]{2,1,0:T(1,128)S(1)}, f32[10,1,64]{2,1,0:T(1,128)S(1)}, u32[]{:S(2)}, u32[]{:S(2)}) collective-permute-start(f32[10,1,64]{2,1,0:T(1,128)S(1)} %get-tuple-element.224), channel_id=1, source_target_pairs={{0,8},{8,16},{16,24},{24,32},{32,40},{40,48},{48,56},{1,9},{9,17},... | collective-permute-start | bytes 7688 | tf_op jit(solution)/shard_map/ppermute | solution.py:23
  131.2 11.6 %collective-permute-start.23 = (f32[18,34,1]{2,1,0:T(8,128)S(1)}, f32[18,34,1]{2,1,0:T(8,128)S(1)}, u32[]{:S(2)}, u32[]{:S(2)}) collective-permute-start(f32[18,34,1]{2,1,0:T(8,128)S(1)} %get-tuple-element.175), channel_id=1, source_target_pairs={{0,1},{1,2},{2,3},{3,4},{4,5},{5,6},{6,7},{8,9},{9,10},{10,11},{11... | collective-permute-start | bytes 7352 | tf_op jit(solution)/shard_map/ppermute | solution.py:23
  137.1 31.7 %collective-permute-start.28 = (f32[10,18,1]{2,1,0:T(8,128)}, f32[10,18,1]{2,1,0:T(8,128)S(1)}, u32[]{:S(2)}, u32[]{:S(2)}) collective-permute-start(f32[10,18,1]{2,1,0:T(8,128)} %get-tuple-element.215), channel_id=1, source_target_pairs={{1,0},{2,1},{3,2},{4,3},{5,4},{6,5},{7,6},{9,8},{10,9},{11,10},{12... | collective-permute-start | bytes 2168 | tf_op jit(solution)/shard_map/ppermute | solution.py:24
  139.0 29.8 %collective-permute-start.29 = (f32[10,18,1]{2,1,0:T(8,128)}, f32[10,18,1]{2,1,0:T(8,128)S(1)}, u32[]{:S(2)}, u32[]{:S(2)}) collective-permute-start(f32[10,18,1]{2,1,0:T(8,128)} %get-tuple-element.214), channel_id=1, source_target_pairs={{0,1},{1,2},{2,3},{3,4},{4,5},{5,6},{6,7},{8,9},{9,10},{10,11},{11... | collective-permute-start | bytes 2168 | tf_op jit(solution)/shard_map/ppermute | solution.py:23
  169.0 12.4 %collective-permute-start.30 = (f32[1,16,64]{2,1,0:T(8,128)S(1)}, f32[1,16,64]{2,1,0:T(8,128)S(1)}, u32[]{:S(2)}, u32[]{:S(2)}) collective-permute-start(f32[1,16,64]{2,1,0:T(8,128)S(1)} %get-tuple-element.233), channel_id=1, source_target_pairs={{64,0},{128,64},{192,128},{65,1},{129,65},{193,129},{66,2},{130,66... | collective-permute-start | bytes 12296 | tf_op jit(solution)/shard_map/ppermute | solution.py:24
  174.6 29.9 %collective-permute-start.44 = (f32[6,1,32]{2,1,0:T(1,128)S(1)}, f32[6,1,32]{2,1,0:T(1,128)S(1)}, u32[]{:S(2)}, u32[]{:S(2)}) collective-permute-start(f32[6,1,32]{2,1,0:T(1,128)S(1)} %get-tuple-element.265), channel_id=1, source_target_pairs={{8,0},{16,8},{24,16},{32,24},{40,32},{48,40},{56,48},{9,1},{17,9},... | collective-permute-start | bytes 2312 | tf_op jit(solution)/shard_map/ppermute | solution.py:24
  175.9 12.3 %collective-permute-start.45 = (f32[6,1,32]{2,1,0:T(1,128)S(1)}, f32[6,1,32]{2,1,0:T(1,128)S(1)}, u32[]{:S(2)}, u32[]{:S(2)}) collective-permute-start(f32[6,1,32]{2,1,0:T(1,128)S(1)} %get-tuple-element.264), channel_id=1, source_target_pairs={{0,8},{8,16},{16,24},{24,32},{32,40},{40,48},{48,56},{1,9},{9,17},... | collective-permute-start | bytes 2312 | tf_op jit(solution)/shard_map/ppermute | solution.py:23
  205.3 11.7 %collective-permute-start.38 = (f32[10,1,64]{2,1,0:T(1,128)S(1)}, f32[10,1,64]{2,1,0:T(1,128)S(1)}, u32[]{:S(2)}, u32[]{:S(2)}) collective-permute-start(f32[10,1,64]{2,1,0:T(1,128)S(1)} %get-tuple-element.221), channel_id=1, source_target_pairs={{8,0},{16,8},{24,16},{32,24},{40,32},{48,40},{56,48},{9,1},{17,9},... | collective-permute-start | bytes 7688 | tf_op jit(solution)/shard_map/ppermute | solution.py:24
  239.2 74.5 %collective-permute-start.51 = (f32[6,1,32]{2,1,0:T(1,128)S(1)}, f32[6,1,32]{2,1,0:T(1,128)S(1)}, u32[]{:S(2)}, u32[]{:S(2)}) collective-permute-start(f32[6,1,32]{2,1,0:T(1,128)S(1)} %get-tuple-element.263), channel_id=1, source_target_pairs={{0,8},{8,16},{16,24},{24,32},{32,40},{40,48},{48,56},{1,9},{9,17},... | collective-permute-start | bytes 2312 | tf_op jit(solution)/shard_map/ppermute | solution.py:23
  (111 other events, 2860.4 us)
where the time goes:
time: 590 us; the launch traced here: 580 us
  starting transfers between devices  282 us (48%)
  blocking collectives  131 us (22%)
  waiting for transfers between devices  64.1 us (11%)
  local copies, waits for them, and re-layouts  57.2 us (10%)
  other arithmetic  41.2 us (7%)
    ppermute x48, starting transfers between devices, extended(): before = lax.ppermute(last, axis, up)  203 us
    ppermute x48, starting transfers between devices, extended(): after = lax.ppermute(leading, axis, down)  79.7 us
    all_gather x1, blocking collectives, on_device(): lax.all_gather(coef_three[None], ('gx', 'gy', 'gz'), axis=0, tiled=True)  68 us
    all_gather x1, blocking collectives, on_device(): lax.all_gather(target_three[None], ('gx', 'gy', 'gz'), axis=0, tiled=True)  63.3 us
    ppermute x48, waiting for transfers between devices, extended(): after = lax.ppermute(leading, axis, down)  42.8 us
    reshape x4, local copies, waits for them, and re-layouts, restrict(): field.reshape(size_x // 2, 2, size_y // 2, 2, size_z // 2, 2)  40.1 us
    ppermute x48, waiting for transfers between devices, extended(): before = lax.ppermute(last, axis, up)  21.3 us
    reduce_sum x6, other arithmetic, restrict(): field.reshape(size_x // 2, 2, size_y // 2, 2, size_z // 2, 2)  16.5 us
  transfers between devices with their start and end apart: 96, of which 33 were waited for; matrix products, arithmetic and copies ran while one was open for 12% of the time, Pallas kernels for 0%

commit v1 on v0

v1 whole, which is shorter than its diff:
```python
import itertools

import jax
import jax.numpy as jnp
import numpy as np
from jax import lax
from jax.experimental import pallas as pl
from jax.experimental.pallas import tpu as pltpu
from jax.sharding import PartitionSpec as P

CHEB = 20
OMEGA = 2.0 / 3.0
CHEB_LOW = 0.1
CHEB_HIGH = 2.0
MESH = pl.DeviceIdType.MESH
F32 = jnp.float32
NX, NY, NZ = 4, 8, 8
SIX = ((1, 0, 0), (-1, 0, 0), (0, 1, 0), (0, -1, 0), (0, 0, 1), (0, 0, -1))
AROUND = sorted(
    (o for o in itertools.product((-1, 0, 1), repeat=3) if o != (0, 0, 0)),
    key=lambda o: -(abs(o[0]) + abs(o[1]) + abs(o[2])),
)
WIDE = sorted(
    (o for o in itertools.product(range(NX), (-1, 0, 1), (-1, 0, 1)) if o != (0, 0, 0)),
    key=lambda o: -((o[0] != 0) + (o[0] == 2) + abs(o[1]) + abs(o[2])),
)


def side(d):
    return 0 if d < 0 else 1


def constants():
    theta, delta = 0.5 * (CHEB_HIGH + CHEB_LOW), 0.5 * (CHEB_HIGH - CHEB_LOW)
    sigma = theta / delta
    rho, out = np.float32(1.0 / sigma), []
    for _ in range(CHEB - 1):
        rho_next = np.float32(1.0 / (2.0 * sigma - rho))
        out += [np.float32(rho_next * rho), np.float32(2.0 * rho_next / delta)]
        rho = rho_next
    return np.array(out, np.float32), theta


def lane(shape):
    return lax.broadcasted_iota(jnp.int32, shape, len(shape) - 1)


def roll(x, by):
    return pltpu.roll(x, by % 128, x.ndim - 1)


def mm(x, m):
    return lax.dot_general(
        x, m, (((1,), (0,)), ((), ())), precision=lax.Precision.HIGHEST, preferred_element_type=F32
    )


def picks(condition, width=128, value=1.0):
    row = lax.broadcasted_iota(jnp.int32, (128, width), 0)
    col = lax.broadcasted_iota(jnp.int32, (128, width), 1)
    return jnp.where(condition(row, col), F32(value), F32(0.0))


def vm(*shape):
    return pltpu.VMEM(shape, F32)


def dma(*shape):
    return pltpu.SemaphoreType.DMA(shape)


def build_scratch():
    s = {}
    for name in ("C0", "V0", "V1", "X0", "VP", "VQ"):
        s[name] = vm(18, 48, 128)
    s.update(WX0=vm(17, 32, 128), WY0=vm(16, 40, 128))
    for name in ("WZM0", "WZP0", "D0", "SD0"):
        s[name] = vm(16, 32, 128)
    s.update(
        YB=vm(5, 2, 16, 1, 128), PZ=vm(5, 32, 128),
        RX=vm(5, 2, 32, 128), RY=vm(5, 2, 16, 1, 128), RZ=vm(5, 2, 32, 128), MZ=vm(5, 32, 128),
        ss0=dma(5, 6), rs0=dma(5, 6),
    )
    s.update(RS0=vm(8, 32, 128), RS1=vm(4, 24, 128), RS2=vm(8, 8, 128), QS=vm(4, 8, 128))
    for k, h in (("c", 5), ("g", 4)):
        s["B1" + k] = vm(8, 16, 128)
        s["PZ1" + k] = vm(16, 128)
        s["RX1" + k] = vm(2, h, 16, 128)
        s["RY1" + k] = vm(2, 8, 8, 128)
        s["RE1" + k] = vm(2, 2, h, 8, 128)
        s["RZ1" + k] = vm(2, 3, 3, 16, 128)
        s["ss1" + k], s["rs1" + k] = dma(26), dma(26)
        s["ZS" + k] = vm(3, 40, 128)
        s["PB2" + k] = vm(8, 128)
        s["S2" + k] = vm(NX, 3, 3, 8, 128)
        s["ss2" + k], s["rs2" + k] = dma(len(WIDE)), dma(len(WIDE))
        s["PB3" + k] = vm(8, 128)
        s["S3" + k] = vm(NZ, 8, 128)
        s["YS" + k] = vm(8, 4, 128)
        s["S4" + k] = vm(NY, 8, 4, 128)
        s["ss3" + k], s["rs3" + k] = dma(NZ), dma(NZ)
        s["ss4" + k], s["rs4" + k] = dma(NY), dma(NY)
    for l in ("1", "2"):
        for name in ("C", "G", "EA", "EB"):
            s[name + l] = vm(18, 40, 128)
        s.update({"WX" + l: vm(17, 24, 128), "WY" + l: vm(16, 32, 128)})
        for name in ("WZM", "WZP", "D", "SD"):
            s[name + l] = vm(16, 24, 128)
    s.update(U2=vm(20, 24, 128), T21=vm(8, 24, 128), D21=vm(8, 24, 128))
    s.update(TA=vm(10, 24, 128), TB=vm(10, 24, 128), DA=vm(10, 48, 128), DB=vm(10, 32, 128))
    s.update(C3=vm(10, 48, 128), T3=vm(8, 32, 128), KA=vm(10, 48, 128), KB=vm(10, 48, 128), ST3=vm(8, 32, 128))
    s.update(WX3=vm(9, 32, 128), WY3=vm(8, 40, 128))
    for name in ("WXM3", "WXP3", "WYM3", "WYP3", "WZM3", "WZP3", "D3", "SD3"):
        s[name] = vm(8, 32, 128)
    s.update(G3=vm(10, 8, 4, 128), R3=vm(8, 16, 128), T32=vm(8, 16, 128), D32=vm(8, 24, 128))
    return s


def kernel(k_ref, g_ref, c_ref, v_ref, o_ref, s):
    gx, gy, gz = (lax.axis_index(a) for a in ("gx", "gy", "gz"))
    one = lambda cond: jnp.where(cond, F32(1.0), F32(0.0))
    mx = {-1: one(gx > 0), 0: F32(1.0), 1: one(gx < NX - 1)}
    my = {-1: one(gy > 0), 0: F32(1.0), 1: one(gy < NY - 1)}
    mz = {-1: one(gz > 0), 0: F32(1.0), 1: one(gz < NZ - 1)}
    started = []

    def target(o):
        return (lax.rem(gx + o[0] + NX, NX), lax.rem(gy + o[1] + NY, NY), lax.rem(gz + o[2] + NZ, NZ))

    def send(src, dst, ss, rs, o):
        copy = pltpu.make_async_remote_copy(
            src_ref=src, dst_ref=dst, send_sem=ss, recv_sem=rs, device_id=target(o), device_id_type=MESH
        )
        copy.start()
        started.append(copy)
        return copy

    def arrive(copies):
        for copy in copies:
            copy.wait_recv()

    barrier = pltpu.get_barrier_semaphore()
    for o in SIX:
        pl.semaphore_signal(barrier, inc=1, device_id=target(o), device_id_type=MESH)

    def pack_fine(plane, k, p, acc):
        s["YB"][k, 0, p] = plane[0:1]
        s["YB"][k, 1, p] = plane[31:32]
        at = lane((32, 128))
        mine = (at == (2 * p) % 128) | (at == (2 * p - 1) % 128)
        moved = roll(plane, 2 * p)
        return jnp.where(mine, moved, acc)

    def send_fine(low, high, k):
        out = []
        ss, rs = s["ss0"], s["rs0"]
        yb, rx, ry, rz = s["YB"], s["RX"], s["RY"], s["RZ"]
        out.append(send(yb.at[k, 1], ry.at[k, 0], ss.at[k, 0], rs.at[k, 0], (0, 1, 0)))
        out.append(send(yb.at[k, 0], ry.at[k, 1], ss.at[k, 1], rs.at[k, 1], (0, -1, 0)))
        out.append(send(high, rx.at[k, 0], ss.at[k, 2], rs.at[k, 2], (1, 0, 0)))
        out.append(send(low, rx.at[k, 1], ss.at[k, 3], rs.at[k, 3], (-1, 0, 0)))
        out.append(send(s["PZ"].at[k], rz.at[k, 0], ss.at[k, 4], rs.at[k, 4], (0, 0, 1)))
        out.append(send(s["PZ"].at[k], rz.at[k, 1], ss.at[k, 5], rs.at[k, 5], (0, 0, -1)))
        return out

    def take_fine(v, k, copies):
        arrive(copies)
        v[0, 8:40, :] = s["RX"][k, 0] * mx[-1]
        v[17, 8:40, :] = s["RX"][k, 1] * mx[1]
        v[1:17, 7:8, :] = s["RY"][k, 0] * my[-1]
        v[1:17, 40:41, :] = s["RY"][k, 1] * my[1]
        odd = lane((32, 128)) % 2 == 1
        s["MZ"][k] = jnp.where(odd, roll(s["RZ"][k, 1], -1) * mz[1], roll(s["RZ"][k, 0], 1) * mz[-1])

    def fine_z(k, extra=None):
        def get(p, v):
            at = lane((32, 128))
            edge = roll(s["MZ"][k], -2 * p)
            if extra is not None:
                edge = edge + extra(p)
            return jnp.where(at == 0, edge, roll(v, 1)), jnp.where(at == 127, edge, roll(v, -1))

        return get

    def plain_z(p, v):
        return roll(v, 1), roll(v, -1)

    def closed_z(p, v):
        at = lane(v.shape)
        return jnp.where(at == 0, 0.0, roll(v, 1)), jnp.where(at == 127, 0.0, roll(v, -1))

    def weights(l, n, rows, scale, zs):
        c, wx, wy = s["C" + l], s["WX" + l], s["WY" + l]
        h = F32(0.5 * scale)
        for p in range(n + 1):
            wx[p] = h * (c[p, 8 : 8 + rows, :] + c[p + 1, 8 : 8 + rows, :])
        for p in range(n):
            wy[p] = h * (c[p + 1, 8 : 16 + rows, :] + c[p + 1, 7 : 15 + rows, :])
            mid = c[p + 1, 8 : 8 + rows, :]
            zm, zp = zs(p, mid)
            wzm, wzp = h * (mid + zm), h * (mid + zp)
            d = wx[p] + wx[p + 1] + wy[p, 0:rows] + wy[p, 1 : rows + 1] + wzm + wzp
            s["WZM" + l][p], s["WZP" + l][p], s["D" + l][p] = wzm, wzp, d
            s["SD" + l][p] = jnp.where(mid > 0, F32(OMEGA) / d, 0.0)

    def gathered(l, v, p, rows, right, zs):
        wx, wy = s["WX" + l], s["WY" + l]
        mid = v[p + 1, 8 : 8 + rows, :]
        zm, zp = zs(p, mid)
        total = right + wx[p] * v[p, 8 : 8 + rows, :] + wx[p + 1] * v[p + 2, 8 : 8 + rows, :]
        total = total + wy[p, 0:rows] * v[p + 1, 7 : 7 + rows, :]
        total = total + wy[p, 1 : rows + 1] * v[p + 1, 9 : 9 + rows, :]
        total = total + s["WZM" + l][p] * zm + s["WZP" + l][p] * zp
        return mid, total

    def swept(l, v, p, rows, right, zs):
        mid, total = gathered(l, v, p, rows, right, zs)
        return mid * F32(1.0 - OMEGA) + s["SD" + l][p] * total

    def residual(l, v, p, rows, right, zs):
        mid, total = gathered(l, v, p, rows, right, zs)
        return total - s["D" + l][p] * mid

    to_one = picks(lambda r, c: r // 2 + 32 == c, value=0.125)
    to_two = [
        picks(lambda r, c, p=p: (c // 32 == p) & (r // 2 == c % 32 + 16), value=0.125) for p in range(4)
    ]
    to_three = [
        picks(lambda r, c, q=q: (c // 16 == q) & (r // 2 == c % 16 + 16) & (c < 64), value=0.125)
        for q in range(4)
    ]

    def restrict_fine(plane, k):
        rs = s["RS0"]
        for q in range(8):
            rs[q] = plane(2 * q) + plane(2 * q + 1)
        half = rs[:, pl.ds(0, 16, stride=2), :] + rs[:, pl.ds(1, 16, stride=2), :]
        block = mm(half.reshape(128, 128), to_one).reshape(8, 16, 128)
        s["B1" + k][...] = block
        at = lane((16, 128))
        acc = jnp.zeros((16, 128), F32)
        for p in range(8):
            acc = jnp.where((at >= 16 * p) & (at < 16 * p + 8), roll(block[p], 16 * p - 32), acc)
            acc = jnp.where((at >= 16 * p + 8) & (at < 16 * p + 16), roll(block[p], 16 * p + 8 - 88), acc)
        s["PZ1" + k][...] = acc

    def restrict_one(plane, first, k):
        rs = s["RS1"]
        rows = 24 if first == 4 else 16
        for q in range(4):
            rs[q, 0:rows] = plane(2 * q) + plane(2 * q + 1)
        half = rs[:, pl.ds(first, 8, stride=2), :] + rs[:, pl.ds(first + 1, 8, stride=2), :]
        s["PB2" + k][...] = sum(mm(half[p], to_two[p]) for p in range(4))

    def restrict_two(plane, k):
        rs, qs = s["RS2"], s["QS"]
        for q in range(8):
            rs[q] = plane(2 * q) + plane(2 * q + 1)
        half = rs[:, pl.ds(0, 4, stride=2), :] + rs[:, pl.ds(1, 4, stride=2), :]
        for q in range(4):
            qs[q, 0:4] = half[2 * q]
            qs[q, 4:8] = half[2 * q + 1]
        s["PB3" + k][...] = sum(mm(qs[q], to_three[q]) for q in range(4))

    def send_one(k, h):
        out = []
        b, pz = s["B1" + k], s["PZ1" + k]
        for i, (dx, dy, dz) in enumerate(AROUND):
            if dz:
                src, dst = pz, s["RZ1" + k].at[side(-dz), 1 - dx, 1 - dy]
            else:
                xs = pl.ds(8 - h, h) if dx > 0 else pl.ds(0, h)
                ys = pl.ds(8, 8) if dy > 0 else pl.ds(0, 8)
                if dx and dy:
                    src, dst = b.at[xs, ys], s["RE1" + k].at[side(-dx), side(-dy)]
                elif dx:
                    src, dst = b.at[xs], s["RX1" + k].at[side(-dx)]
                else:
                    src, dst = b.at[:, ys], s["RY1" + k].at[side(-dy)]
            out.append(send(src, dst, s["ss1" + k].at[i], s["rs1" + k].at[i], (dx, dy, dz)))
        return out

    def take_one(e, k, h, copies):
        arrive(copies)
        b, rx, ry, re, rz, zs = (s[n + k] for n in ("B1", "RX1", "RY1", "RE1", "RZ1", "ZS"))
        first = lane((16, 128)) % 16 >= 8

        def beside(dx, dy):
            left = rz[0, 1 + dx, 1 + dy] * mz[-1]
            right = roll(rz[1, 1 + dx, 1 + dy], 80) * mz[1]
            return jnp.where(first, left, right) * (mx[dx] * my[dy])

        for dx in (-1, 0, 1):
            zs[1 + dx, 12:28] = beside(dx, 0)
            zs[1 + dx, 12 - h : 12] = beside(dx, -1)[16 - h : 16]
            zs[1 + dx, 28 : 28 + h] = beside(dx, 1)[0:h]
            count, base, start = (8, 5, 0) if dx == 0 else ((h, 5 - h, 8 - h) if dx < 0 else (h, 13, 0))
            planes = pl.ds(base, count)
            if dx == 0:
                e[planes, 12:28, :] = b[...]
                e[planes, 12 - h : 12, :] = ry[0, :, 8 - h : 8, :] * my[-1]
                e[planes, 28 : 28 + h, :] = ry[1, :, 0:h, :] * my[1]
            else:
                e[planes, 12:28, :] = rx[side(dx)] * mx[dx]
                e[planes, 12 - h : 12, :] = re[side(dx), 0, :, 8 - h : 8, :] * (mx[dx] * my[-1])
                e[planes, 28 : 28 + h, :] = re[side(dx), 1, :, 0:h, :] * (mx[dx] * my[1])
            lo, hi = (8, 32) if h == 4 else (0, 40)
            at = lane((hi - lo, 128))
            halo = ((at >= 24) & (at < 32)) | ((at >= 96) & (at < 104))
            for i in range(count):
                moved = roll(zs[1 + dx, lo:hi], 16 - 16 * (start + i))
                e[base + i, lo:hi, :] = jnp.where(halo, moved, e[base + i, lo:hi, :])

    def send_two(k):
        out = []
        for i, (a, dy, dz) in enumerate(WIDE):
            dst = s["S2" + k].at[gx, 1 - dy, 1 - dz]
            out.append(send(s["PB2" + k], dst, s["ss2" + k].at[i], s["rs2" + k].at[i], (a, dy, dz)))
        s["S2" + k][gx, 1, 1] = s["PB2" + k][...]
        return out

    def take_two(e, k, copies):
        arrive(copies)
        at = lane((8, 128)) // 32
        for x in range(NX):
            for dy in (-1, 0, 1):
                blocks = [s["S2" + k][x, 1 + dy, 1 + dz] * (my[dy] * mz[dz]) for dz in (-1, 0, 1)]
                for p in range(4):
                    val = jnp.zeros((8, 128), F32)
                    for z in range(3):
                        val = jnp.where(at == z, roll(blocks[z], 32 * (z - p)), val)
                    e[1 + 4 * x + p, 16 + 8 * dy : 24 + 8 * dy, :] = val

    def send_z(k):
        out = []
        for a in range(1, NZ):
            dst = s["S3" + k].at[gz]
            out.append(send(s["PB3" + k], dst, s["ss3" + k].at[a], s["rs3" + k].at[a], (0, 0, a)))
        s["S3" + k][gz] = s["PB3" + k][...]
        return out

    def pass_y(k, copies):
        arrive(copies)
        at = lane((8, 128)) // 16
        for q in range(4):
            val = jnp.zeros((8, 128), F32)
            for j in range(NZ):
                val = jnp.where(at == j, roll(s["S3" + k][j], 16 * (j - q)), val)
            s["YS" + k][2 * q] = val[0:4]
            s["YS" + k][2 * q + 1] = val[4:8]
        out = []
        for a in range(1, NY):
            dst = s["S4" + k].at[gy]
            out.append(send(s["YS" + k], dst, s["ss4" + k].at[a], s["rs4" + k].at[a], (0, a, 0)))
        s["S4" + k][gy] = s["YS" + k][...]
        return out

    for name in ("C1", "G1", "EA1", "EB1", "C2", "G2", "EA2", "EB2"):
        s[name][...] = jnp.zeros((18, 40, 128), F32)
    for name in ("C3", "KA", "KB"):
        s[name][...] = jnp.zeros((10, 48, 128), F32)
    s["ZSc"][...] = jnp.zeros((3, 40, 128), F32)
    s["U2"][...] = jnp.zeros((20, 24, 128), F32)
    s["R3"][...] = jnp.zeros((8, 16, 128), F32)
    s["G3"][...] = jnp.zeros((10, 8, 4, 128), F32)
    for k, ref, v in ((0, c_ref, "C0"), (1, v_ref, "V0")):
        acc = jnp.zeros((32, 128), F32)
        for p in range(16):
            plane = ref[p]
            s[v][p + 1, 8:40, :] = plane
            acc = pack_fine(plane, k, p, acc)
        s["PZ"][k] = acc
    pl.semaphore_wait(barrier, len(SIX))

    cc = send_fine(c_ref.at[0], c_ref.at[15], 0)
    vv = send_fine(v_ref.at[0], v_ref.at[15], 1)
    restrict_fine(lambda p: c_ref[p], "c")
    restrict_one(lambda p: s["B1c"][p], 0, "c")
    take_fine(s["C0"], 0, cc)
    weights("0", 16, 32, 1.0, fine_z(0))
    take_fine(s["V0"], 1, vv)

    def sweep_fine(src, dst, zs, k):
        acc = jnp.zeros((32, 128), F32)
        for p in range(16):
            new = swept("0", s[src], p, 32, g_ref[p], zs)
            s[dst][p + 1, 8:40, :] = new
            acc = pack_fine(new, k, p, acc)
        s["PZ"][k] = acc
        return send_fine(s[dst].at[1, 8:40], s[dst].at[16, 8:40], k)

    copies = sweep_fine("V0", "V1", fine_z(1), 2)
    take_fine(s["V1"], 2, copies)
    copies = sweep_fine("V1", "X0", fine_z(2), 3)
    c_one = send_one("c", 5)
    take_fine(s["X0"], 3, copies)
    restrict_fine(lambda p: residual("0", s["X0"], p, 32, g_ref[p], fine_z(3)), "g")

    g_one = send_one("g", 4)
    take_one(s["C1"], "c", 5, c_one)
    c_two = send_two("c")
    weights("1", 16, 24, 0.25, plain_z)
    take_one(s["G1"], "g", 4, g_one)

    def begin(l):
        for p in range(16):
            s["EA" + l][p + 1, 8:32, :] = s["SD" + l][p] * s["G" + l][p + 1, 8:32, :]

    def sweep(l, src, dst):
        for p in range(16):
            right = s["G" + l][p + 1, 8:32, :]
            s[dst][p + 1, 8:32, :] = swept(l, s[src], p, 24, right, plain_z)

    def left(l, src):
        return lambda p: residual(l, s[src], p, 24, s["G" + l][p + 1, 8:32, :], plain_z)

    begin("1")
    sweep("1", "EA1", "EB1")
    rest = left("1", "EB1")
    restrict_one(lambda p: rest(p + 4), 4, "g")

    g_two = send_two("g")
    take_two(s["C2"], "c", c_two)
    restrict_two(lambda p: s["C2"][p + 1, 16:24, :], "c")
    c_z = send_z("c")
    weights("2", 16, 24, 0.0625, plain_z)
    take_two(s["G2"], "g", g_two)
    begin("2")
    sweep("2", "EA2", "EB2")
    rest2 = left("2", "EB2")
    restrict_two(lambda p: rest2(p)[8:16], "g")

    g_z = send_z("g")
    c_y = pass_y("c", c_z)
    g_y = pass_y("g", g_z)
    arrive(c_y)
    for g in range(NY):
        s["C3"][1:9, 8 + 4 * g : 12 + 4 * g, :] = s["S4c"][g]
    weights("3", 8, 32, 0.015625, closed_z)
    at = lane((32, 128))
    for p in range(8):
        inv = F32(1.0) / s["D3"][p]
        s["SD3"][p] = inv
        s["WXM3"][p] = s["WX3"][p] * inv
        s["WXP3"][p] = s["WX3"][p + 1] * inv
        s["WYM3"][p] = s["WY3"][p, 0:32] * inv
        s["WYP3"][p] = s["WY3"][p, 1:33] * inv
        s["WZM3"][p] = jnp.where(at == 0, 0.0, s["WZM3"][p] * inv)
        s["WZP3"][p] = jnp.where(at == 127, 0.0, s["WZP3"][p] * inv)
    arrive(g_y)
    for g in range(NY):
        s["T3"][:, 4 * g : 4 * g + 4, :] = s["S4g"][g]
    theta = constants()[1]
    for p in range(8):
        t = s["T3"][p] * s["SD3"][p]
        s["T3"][p] = t
        d = t * F32(1.0 / theta)
        s["ST3"][p] = d
        s["KA"][p + 1, 8:40, :] = d

    def cheb(src, dst, i):
        a, b = k_ref[2 * i], k_ref[2 * i + 1]
        v = s[src]
        for p in range(8):
            e = v[p + 1, 8:40, :]
            r = s["T3"][p] - e + s["WXM3"][p] * v[p, 8:40, :] + s["WXP3"][p] * v[p + 2, 8:40, :]
            r = r + s["WYM3"][p] * v[p + 1, 7:39, :] + s["WYP3"][p] * v[p + 1, 9:41, :]
            r = r + s["WZM3"][p] * roll(e, 1) + s["WZP3"][p] * roll(e, -1)
            d = a * s["ST3"][p] + b * r
            s["ST3"][p] = d
            s[dst][p + 1, 8:40, :] = e + d

    def two(i, carry):
        cheb("KA", "KB", 2 * i)
        cheb("KB", "KA", 2 * i + 1)
        return carry

    lax.fori_loop(0, (CHEB - 1) // 2, two, 0)
    cheb("KA", "KB", CHEB - 2)

    for g in range(NY):
        s["G3"][g + 1] = s["KB"][1:9, 8 + 4 * g : 12 + 4 * g, :]
    for j in range(3):
        s["R3"][:, 4 * j : 4 * j + 4, :] = s["G3"][gy + j]
    from_three = picks(lambda r, c: (r == 16 * gz - 16 + c // 2) & (c < 96))
    s["T32"][...] = mm(s["R3"][...].reshape(128, 128), from_three).reshape(8, 16, 128)
    for o in (0, 1):
        s["D32"][:, pl.ds(o, 12, stride=2), :] = s["T32"][:, 0:12, :]
    for p in range(16):
        s["EA2"][p + 1, 8:32, :] = s["EB2"][p + 1, 8:32, :] + s["D32"][p // 2]
    sweep("2", "EA2", "EB2")
    for p in range(16):
        right = s["G2"][p + 1, 8:32, :]
        s["U2"][p + 2] = swept("2", s["EB2"], p, 24, right, plain_z)

    from_two = picks(lambda r, c: (r == 16 + c // 2) & (c >= 24) & (c < 104))
    part = s["U2"][pl.ds(4 * gx, 8)]
    s["T21"][...] = mm(part.reshape(192, 128), from_two).reshape(8, 24, 128)
    for o in (0, 1):
        s["D21"][:, pl.ds(o, 12, stride=2), :] = s["T21"][:, 6:18, :]
    for p in range(16):
        s["EA1"][p + 1, 8:32, :] = s["EB1"][p + 1, 8:32, :] + s["D21"][p // 2]
    sweep("1", "EA1", "EB1")
    sweep("1", "EB1", "EA1")

    from_one = picks(
        lambda r, c: ((c < 128) & (r == 32 + c // 2)) | ((c == 128) & (r == 31)) | ((c == 255) & (r == 96)), 256
    )
    wide = mm(s["EA1"][4:14, 8:32, :].reshape(240, 128), from_one)
    s["TA"][...] = wide[:, 0:128].reshape(10, 24, 128)
    s["TB"][...] = wide[:, 128:256].reshape(10, 24, 128)
    for o in (0, 1):
        s["DA"][:, pl.ds(8 + o, 16, stride=2), :] = s["TA"][:, 4:20, :]
        s["DB"][:, pl.ds(o, 16, stride=2), :] = s["TB"][:, 4:20, :]
    for i in range(18):
        j = (i + 1) // 2
        s["VP"][i, 8:40, :] = s["X0"][i, 8:40, :] + s["DA"][j, 8:40, :]
        if 0 < i < 17:
            s["VP"][i, 7:8, :] = s["X0"][i, 7:8, :] + s["TA"][j, 3:4, :]
            s["VP"][i, 40:41, :] = s["X0"][i, 40:41, :] + s["TA"][j, 20:21, :]
    copies = sweep_fine("VP", "VQ", fine_z(3, lambda p: s["DB"][(p + 2) // 2]), 4)
    take_fine(s["VQ"], 4, copies)
    for p in range(16):
        o_ref[p] = swept("0", s["VQ"], p, 32, g_ref[p], fine_z(4))
    for copy in started:
        copy.wait_send()


def on_device(right_side, coefficient, guess):
    table = jnp.asarray(constants()[0])
    vmem = pl.BlockSpec(memory_space=pltpu.VMEM)
    return pl.pallas_call(
        kernel,
        out_shape=jax.ShapeDtypeStruct((16, 32, 128), F32),
        in_specs=[pl.BlockSpec(memory_space=pltpu.SMEM), vmem, vmem, vmem],
        out_specs=vmem,
        scratch_shapes=[build_scratch()],
        compiler_params=pltpu.CompilerParams(
            collective_id=0, has_side_effects=True, vmem_limit_bytes=56 * 2**20
        ),
    )(table, right_side, coefficient, guess)


def solution(mesh):
    spec = P("gx", "gy", "gz")
    return jax.shard_map(on_device, mesh=mesh, in_specs=(spec, spec, spec), out_specs=spec, check_vma=False)
```

time: 590 us -> 56.5 us (0.10); the launches traced: 580 us -> 56.3 us
  starting transfers between devices: 282 us -> 0 us
  blocking collectives: 131 us -> 0 us
  waiting for transfers between devices: 64.1 us -> 0 us
  local copies, waits for them, and re-layouts: 57.2 us -> 1.67 us
  Pallas kernels: 0 us -> 54.6 us
  other arithmetic: 41.2 us -> 0 us
    ppermute x96 -> x0, starting transfers between devices: 282 us -> none  [the longest x48 203 us: extended(): before = lax.ppermute(last, axis, up)]
    all_gather x2 -> x0, blocking collectives: 131 us -> none  [the longest x1 68 us: on_device(): lax.all_gather(coef_three[None], ('gx', 'gy', 'gz'), axis=0, tiled=True)]
    ppermute x96 -> x0, waiting for transfers between devices: 64.1 us -> none  [the longest x48 42.8 us: extended(): after = lax.ppermute(leading, axis, down)]
    pallas_call x0 -> x1, Pallas kernels: none -> 54.6 us  [on_device(): pl.pallas_call(kernel, out_shape=jax.ShapeDtypeStruct((16, 32, 128), F32)...]
    reshape x12 -> x0, local copies, waits for them, and re-layouts: 43.9 us -> none  [the longest x4 40.1 us: restrict(): field.reshape(size_x // 2, 2, size_y // 2, 2, size_z // 2, 2)]
    add x32 -> x0, other arithmetic: 17 us -> none  [the longest x10 12.1 us: smooth_once(): field + OMEGA * (target - operate(halo_fn(field), padded_coef, scale)) /...]
    reduce_sum x6 -> x0, other arithmetic: 16.5 us -> none  [restrict(): field.reshape(size_x // 2, 2, size_y // 2, 2, size_z // 2, 2)]
    slice x39 -> x0, local copies, waits for them, and re-layouts: 6.96 us -> none  [the longest x21 3.86 us: extended(): last = lax.slice_in_dim(shard, length - width, length, axis=dim)]
  transfers between devices with their start and end apart: 96 -> 0, of which waited for: 33 -> 0; matrix products, arithmetic and copies ran while one was open for 12% -> 0% of each run, Pallas kernels for 0% -> 0%
where the time goes in v1:
time: 56.5 us; the launch traced here: 56.3 us
  Pallas kernels  54.6 us (97%)
  local copies, waits for them, and re-layouts  1.67 us (3%)
    pallas_call x1, Pallas kernels, on_device(): pl.pallas_call(kernel, out_shape=jax.ShapeDtypeStruct((16, 32, 128), F32)...  54.6 us
    unnamed x1, local copies, waits for them, and re-layouts  1.67 us

profile of v1, /device:TPU:1, one launch (start us, length us, event | category | flops | bytes accessed | tf_op | source)
XLA Modules:
  0.0 56.3 jit_solution(3446233447525811585)
XLA Ops:
  0.0 54.6 %shard_map.46 = f32[16,32,128]{2,1,0:T(8,128)} custom-call(f32[38]{0:T(128)} %constant.2.clone.k_ref, f32[16,32,128]{2,1,0:T(8,128)} %g_ref.1, f32[16,32,128]{2,1,0:T(8,128)} %c_ref.1, f32[16,32,128]{2,1,0:T(8,128)} %v_ref.1), custom_call_target="tpu_custom_call" | custom-call | tf_op jit(solution)/shard_map/pallas_call | solution.py:532
  54.7 1.7 %copy.6 = f32[16,32,128]{2,1,0:T(8,128)} copy(f32[16,32,128]{2,1,0:T(8,128)} %shard_map.46) | data formatting | bytes 524288

commit v2 on v1

--- a/solution.py
+++ b/solution.py
@@ -24,6 +24,12 @@
     (o for o in itertools.product(range(NX), (-1, 0, 1), (-1, 0, 1)) if o != (0, 0, 0)),
     key=lambda o: -((o[0] != 0) + (o[0] == 2) + abs(o[1]) + abs(o[2])),
 )
+CHIPS = sorted(
+    (o for o in itertools.product((0,), range(NY), range(0, NZ, 2)) if o != (0, 0, 0)),
+    key=lambda o: -(min(o[1], NY - o[1]) + min(o[2], NZ - o[2]) // 2),
+)
+NEAR = {(o[0], o[1] % NY, o[2] % NZ) for o in SIX}
+FAR = [o for o in CHIPS if o not in NEAR]
 
 
 def side(d):
@@ -77,9 +83,9 @@
     for name in ("WZM0", "WZP0", "D0", "SD0"):
         s[name] = vm(16, 32, 128)
     s.update(
-        YB=vm(5, 2, 16, 1, 128), PZ=vm(5, 32, 128),
-        RX=vm(5, 2, 32, 128), RY=vm(5, 2, 16, 1, 128), RZ=vm(5, 2, 32, 128), MZ=vm(5, 32, 128),
-        ss0=dma(5, 6), rs0=dma(5, 6),
+        YB=vm(2, 5, 16, 1, 128), PZ=vm(5, 32, 128),
+        RX=vm(5, 2, 32, 128), RY=vm(2, 5, 16, 1, 128), RZ=vm(2, 5, 32, 128), MZ=vm(5, 32, 128),
+        ss0=dma(5, 6), rs0=dma(5, 6), hs=dma(8), GV=vm(16, 32, 128), OV=vm(16, 32, 128),
     )
     s.update(RS0=vm(8, 32, 128), RS1=vm(4, 24, 128), RS2=vm(8, 8, 128), QS=vm(4, 8, 128))
     for k, h in (("c", 5), ("g", 4)):
@@ -95,17 +101,18 @@
         s["S2" + k] = vm(NX, 3, 3, 8, 128)
         s["ss2" + k], s["rs2" + k] = dma(len(WIDE)), dma(len(WIDE))
         s["PB3" + k] = vm(8, 128)
-        s["S3" + k] = vm(NZ, 8, 128)
-        s["YS" + k] = vm(8, 4, 128)
-        s["S4" + k] = vm(NY, 8, 4, 128)
-        s["ss3" + k], s["rs3" + k] = dma(NZ), dma(NZ)
-        s["ss4" + k], s["rs4" + k] = dma(NY), dma(NY)
+        s["S3" + k] = vm(8, 128)
+        s["YS" + k] = vm(8, 128)
+        s["S4" + k] = vm(NY, NZ // 2, 8, 128)
+        s["ss3" + k], s["rs3" + k] = dma(1), dma(1)
+        s["ss4" + k], s["rs4" + k] = dma(len(CHIPS)), dma(len(CHIPS))
     for l in ("1", "2"):
         for name in ("C", "G", "EA", "EB"):
             s[name + l] = vm(18, 40, 128)
         s.update({"WX" + l: vm(17, 24, 128), "WY" + l: vm(16, 32, 128)})
         for name in ("WZM", "WZP", "D", "SD"):
             s[name + l] = vm(16, 24, 128)
+    s["K"] = pltpu.SMEM((2 * (CHEB - 1),), F32)
     s.update(U2=vm(20, 24, 128), T21=vm(8, 24, 128), D21=vm(8, 24, 128))
     s.update(TA=vm(10, 24, 128), TB=vm(10, 24, 128), DA=vm(10, 48, 128), DB=vm(10, 32, 128))
     s.update(C3=vm(10, 48, 128), T3=vm(8, 32, 128), KA=vm(10, 48, 128), KB=vm(10, 48, 128), ST3=vm(8, 32, 128))
@@ -116,61 +123,95 @@
     return s
 
 
-def kernel(k_ref, g_ref, c_ref, v_ref, o_ref, s):
+def kernel(g_hbm, c_hbm, v_hbm, o_ref, s):
     gx, gy, gz = (lax.axis_index(a) for a in ("gx", "gy", "gz"))
-    one = lambda cond: jnp.where(cond, F32(1.0), F32(0.0))
-    mx = {-1: one(gx > 0), 0: F32(1.0), 1: one(gx < NX - 1)}
-    my = {-1: one(gy > 0), 0: F32(1.0), 1: one(gy < NY - 1)}
-    mz = {-1: one(gz > 0), 0: F32(1.0), 1: one(gz < NZ - 1)}
+    here = {
+        0: {-1: gx > 0, 1: gx < NX - 1},
+        1: {-1: gy > 0, 1: gy < NY - 1},
+        2: {-1: gz > 0, 1: gz < NZ - 1},
+    }
+    core = lax.rem(gz, 2)
     started = []
+
+    def exists(o, axes=(0, 1, 2)):
+        cond = None
+        for axis in axes:
+            if o[axis]:
+                cond = here[axis][o[axis]] if cond is None else cond & here[axis][o[axis]]
+        return cond
+
+    def keep(x, *o, axes=(0, 1, 2)):
+        cond = exists(o, axes)
+        return x if cond is None else jnp.where(cond, x, 0.0)
+
+    def when(cond, act):
+        if cond is None:
+            act()
+        else:
+            pl.when(cond)(act)
 
     def target(o):
         return (lax.rem(gx + o[0] + NX, NX), lax.rem(gy + o[1] + NY, NY), lax.rem(gz + o[2] + NZ, NZ))
 
-    def send(src, dst, ss, rs, o):
+    def send(src, dst, ss, rs, o, axes=(0, 1, 2), to=None):
         copy = pltpu.make_async_remote_copy(
-            src_ref=src, dst_ref=dst, send_sem=ss, recv_sem=rs, device_id=target(o), device_id_type=MESH
+            src_ref=src, dst_ref=dst, send_sem=ss, recv_sem=rs,
+            device_id=target(o) if to is None else to, device_id_type=MESH,
         )
-        copy.start()
-        started.append(copy)
-        return copy
+        out = exists(o, axes)
+        when(out, copy.start)
+        started.append((copy, out))
+        return copy, exists(tuple(-d for d in o), axes)
 
     def arrive(copies):
-        for copy in copies:
-            copy.wait_recv()
+        for copy, cond in copies:
+            when(cond, copy.wait_recv)
 
     barrier = pltpu.get_barrier_semaphore()
     for o in SIX:
         pl.semaphore_signal(barrier, inc=1, device_id=target(o), device_id_type=MESH)
+    main = (pl.ds(1, 16), pl.ds(8, 32))
+    loads = [
+        pltpu.make_async_copy(c_hbm, s["C0"].at[main], s["hs"].at[0]),
+        pltpu.make_async_copy(v_hbm, s["V0"].at[main], s["hs"].at[1]),
+        pltpu.make_async_copy(g_hbm, s["GV"], s["hs"].at[2]),
+    ]
+    for load in loads:
+        load.start()
+    for o in FAR:
+        pl.semaphore_signal(barrier, inc=1, device_id=target(o), device_id_type=MESH)
 
     def pack_fine(plane, k, p, acc):
-        s["YB"][k, 0, p] = plane[0:1]
-        s["YB"][k, 1, p] = plane[31:32]
+        s["YB"][0, k, p] = plane[0:1]
+        s["YB"][1, k, p] = plane[31:32]
         at = lane((32, 128))
         mine = (at == (2 * p) % 128) | (at == (2 * p - 1) % 128)
-        moved = roll(plane, 2 * p)
-        return jnp.where(mine, moved, acc)
-
-    def send_fine(low, high, k):
+        return jnp.where(mine, roll(plane, 2 * p), acc)
+
+    def send_fine(names, k):
         out = []
         ss, rs = s["ss0"], s["rs0"]
-        yb, rx, ry, rz = s["YB"], s["RX"], s["RY"], s["RZ"]
-        out.append(send(yb.at[k, 1], ry.at[k, 0], ss.at[k, 0], rs.at[k, 0], (0, 1, 0)))
-        out.append(send(yb.at[k, 0], ry.at[k, 1], ss.at[k, 1], rs.at[k, 1], (0, -1, 0)))
-        out.append(send(high, rx.at[k, 0], ss.at[k, 2], rs.at[k, 2], (1, 0, 0)))
-        out.append(send(low, rx.at[k, 1], ss.at[k, 3], rs.at[k, 3], (-1, 0, 0)))
-        out.append(send(s["PZ"].at[k], rz.at[k, 0], ss.at[k, 4], rs.at[k, 4], (0, 0, 1)))
-        out.append(send(s["PZ"].at[k], rz.at[k, 1], ss.at[k, 5], rs.at[k, 5], (0, 0, -1)))
+        yb, rx, ry, rz, pz = s["YB"], s["RX"], s["RY"], s["RZ"], s["PZ"]
+        ks = pl.ds(k, len(names))
+        out.append(send(yb.at[1, ks], ry.at[0, ks], ss.at[k, 0], rs.at[k, 0], (0, 1, 0)))
+        out.append(send(yb.at[0, ks], ry.at[1, ks], ss.at[k, 1], rs.at[k, 1], (0, -1, 0)))
+        for i, name in enumerate(names):
+            low, high = s[name].at[1, pl.ds(8, 32)], s[name].at[16, pl.ds(8, 32)]
+            out.append(send(high, rx.at[k + i, 0], ss.at[k + i, 2], rs.at[k + i, 2], (1, 0, 0)))
+            out.append(send(low, rx.at[k + i, 1], ss.at[k + i, 3], rs.at[k + i, 3], (-1, 0, 0)))
+        out.append(send(pz.at[ks], rz.at[0, ks], ss.at[k, 4], rs.at[k, 4], (0, 0, 1)))
+        out.append(send(pz.at[ks], rz.at[1, ks], ss.at[k, 5], rs.at[k, 5], (0, 0, -1)))
         return out
 
-    def take_fine(v, k, copies):
-        arrive(copies)
-        v[0, 8:40, :] = s["RX"][k, 0] * mx[-1]
-        v[17, 8:40, :] = s["RX"][k, 1] * mx[1]
-        v[1:17, 7:8, :] = s["RY"][k, 0] * my[-1]
-        v[1:17, 40:41, :] = s["RY"][k, 1] * my[1]
+    def take_fine(name, k):
+        v = s[name]
+        v[0, 8:40, :] = keep(s["RX"][k, 0], -1, 0, 0)
+        v[17, 8:40, :] = keep(s["RX"][k, 1], 1, 0, 0)
+        v[1:17, 7:8, :] = keep(s["RY"][0, k], 0, -1, 0)
+        v[1:17, 40:41, :] = keep(s["RY"][1, k], 0, 1, 0)
         odd = lane((32, 128)) % 2 == 1
-        s["MZ"][k] = jnp.where(odd, roll(s["RZ"][k, 1], -1) * mz[1], roll(s["RZ"][k, 0], 1) * mz[-1])
+        right, left = keep(s["RZ"][1, k], 0, 0, 1), keep(s["RZ"][0, k], 0, 0, -1)
+        s["MZ"][k] = jnp.where(odd, roll(right, -1), roll(left, 1))
 
     def fine_z(k, extra=None):
         def get(p, v):
@@ -226,7 +267,7 @@
         picks(lambda r, c, p=p: (c // 32 == p) & (r // 2 == c % 32 + 16), value=0.125) for p in range(4)
     ]
     to_three = [
-        picks(lambda r, c, q=q: (c // 16 == q) & (r // 2 == c % 16 + 16) & (c < 64), value=0.125)
+        picks(lambda r, c, q=q: (c // 16 == 2 * q + core) & (r // 2 == c % 16 + 16), value=0.125)
         for q in range(4)
     ]
 
@@ -286,9 +327,9 @@
         first = lane((16, 128)) % 16 >= 8
 
         def beside(dx, dy):
-            left = rz[0, 1 + dx, 1 + dy] * mz[-1]
-            right = roll(rz[1, 1 + dx, 1 + dy], 80) * mz[1]
-            return jnp.where(first, left, right) * (mx[dx] * my[dy])
+            left = keep(rz[0, 1 + dx, 1 + dy], dx, dy, -1)
+            right = roll(keep(rz[1, 1 + dx, 1 + dy], dx, dy, 1), 80)
+            return jnp.where(first, left, right)
 
         for dx in (-1, 0, 1):
             zs[1 + dx, 12:28] = beside(dx, 0)
@@ -298,12 +339,12 @@
             planes = pl.ds(base, count)
             if dx == 0:
                 e[planes, 12:28, :] = b[...]
-                e[planes, 12 - h : 12, :] = ry[0, :, 8 - h : 8, :] * my[-1]
-                e[planes, 28 : 28 + h, :] = ry[1, :, 0:h, :] * my[1]
+                e[planes, 12 - h : 12, :] = keep(ry[0, :, 8 - h : 8, :], 0, -1, 0)
+                e[planes, 28 : 28 + h, :] = keep(ry[1, :, 0:h, :], 0, 1, 0)
             else:
-                e[planes, 12:28, :] = rx[side(dx)] * mx[dx]
-                e[planes, 12 - h : 12, :] = re[side(dx), 0, :, 8 - h : 8, :] * (mx[dx] * my[-1])
-                e[planes, 28 : 28 + h, :] = re[side(dx), 1, :, 0:h, :] * (mx[dx] * my[1])
+                e[planes, 12:28, :] = keep(rx[side(dx)], dx, 0, 0)
+                e[planes, 12 - h : 12, :] = keep(re[side(dx), 0, :, 8 - h : 8, :], dx, -1, 0)
+                e[planes, 28 : 28 + h, :] = keep(re[side(dx), 1, :, 0:h, :], dx, 1, 0)
             lo, hi = (8, 32) if h == 4 else (0, 40)
             at = lane((hi - lo, 128))
             halo = ((at >= 24) & (at < 32)) | ((at >= 96) & (at < 104))
@@ -315,7 +356,7 @@
         out = []
         for i, (a, dy, dz) in enumerate(WIDE):
             dst = s["S2" + k].at[gx, 1 - dy, 1 - dz]
-            out.append(send(s["PB2" + k], dst, s["ss2" + k].at[i], s["rs2" + k].at[i], (a, dy, dz)))
+            out.append(send(s["PB2" + k], dst, s["ss2" + k].at[i], s["rs2" + k].at[i], (a, dy, dz), (1, 2)))
         s["S2" + k][gx, 1, 1] = s["PB2" + k][...]
         return out
 
@@ -324,37 +365,50 @@
         at = lane((8, 128)) // 32
         for x in range(NX):
             for dy in (-1, 0, 1):
-                blocks = [s["S2" + k][x, 1 + dy, 1 + dz] * (my[dy] * mz[dz]) for dz in (-1, 0, 1)]
+                blocks = [keep(s["S2" + k][x, 1 + dy, 1 + dz], 0, dy, dz) for dz in (-1, 0, 1)]
                 for p in range(4):
                     val = jnp.zeros((8, 128), F32)
                     for z in range(3):
                         val = jnp.where(at == z, roll(blocks[z], 32 * (z - p)), val)
                     e[1 + 4 * x + p, 16 + 8 * dy : 24 + 8 * dy, :] = val
 
-    def send_z(k):
+    def send_core(k):
+        to = (gx, gy, gz + 1 - 2 * core)
+        return [send(s["PB3" + k], s["S3" + k], s["ss3" + k].at[0], s["rs3" + k].at[0], (0, 0, 0), to=to)]
+
+    def send_chips(k, copies):
+        arrive(copies)
+        s["YS" + k][...] = s["PB3" + k][...] + s["S3" + k][...]
         out = []
-        for a in range(1, NZ):
-            dst = s["S3" + k].at[gz]
-            out.append(send(s["PB3" + k], dst, s["ss3" + k].at[a], s["rs3" + k].at[a], (0, 0, a)))
-        s["S3" + k][gz] = s["PB3" + k][...]
+        for i, o in enumerate(CHIPS):
+            dst = s["S4" + k].at[gy, gz // 2]
+            out.append(send(s["YS" + k], dst, s["ss4" + k].at[i], s["rs4" + k].at[i], o, ()))
+        s["S4" + k][gy, gz // 2] = s["YS" + k][...]
         return out
 
-    def pass_y(k, copies):
+    def take_coarse(dst, base, row, k, copies):
         arrive(copies)
-        at = lane((8, 128)) // 16
-        for q in range(4):
-            val = jnp.zeros((8, 128), F32)
-            for j in range(NZ):
-                val = jnp.where(at == j, roll(s["S3" + k][j], 16 * (j - q)), val)
-            s["YS" + k][2 * q] = val[0:4]
-            s["YS" + k][2 * q + 1] = val[4:8]
-        out = []
-        for a in range(1, NY):
-            dst = s["S4" + k].at[gy]
-            out.append(send(s["YS" + k], dst, s["ss4" + k].at[a], s["rs4" + k].at[a], (0, a, 0)))
-        s["S4" + k][gy] = s["YS" + k][...]
-        return out
-
+        at = lane((8, 128)) // 32
+        for g in range(NY):
+            for q in range(4):
+                val = jnp.zeros((8, 128), F32)
+                for j in range(NZ // 2):
+                    val = jnp.where(at == j, roll(s["S4" + k][g, j], 32 * (j - q)), val)
+                rows = slice(row + 4 * g, row + 4 * g + 4)
+                dst[base + 2 * q, rows, :] = val[0:4]
+                dst[base + 2 * q + 1, rows, :] = val[4:8]
+
+    for k, name in ((0, "C0"), (1, "V0")):
+        loads[k].wait()
+        acc = jnp.zeros((32, 128), F32)
+        for p in range(16):
+            acc = pack_fine(s[name][p + 1, 8:40, :], k, p, acc)
+        s["PZ"][k] = acc
+    pl.semaphore_wait(barrier, len(SIX) + len(FAR))
+
+    copies = send_fine(("C0", "V0"), 0)
+    loads[2].wait()
+    g_ref = s["GV"]
     for name in ("C1", "G1", "EA1", "EB1", "C2", "G2", "EA2", "EB2"):
         s[name][...] = jnp.zeros((18, 40, 128), F32)
     for name in ("C3", "KA", "KB"):
@@ -363,22 +417,12 @@
     s["U2"][...] = jnp.zeros((20, 24, 128), F32)
     s["R3"][...] = jnp.zeros((8, 16, 128), F32)
     s["G3"][...] = jnp.zeros((10, 8, 4, 128), F32)
-    for k, ref, v in ((0, c_ref, "C0"), (1, v_ref, "V0")):
-        acc = jnp.zeros((32, 128), F32)
-        for p in range(16):
-            plane = ref[p]
-            s[v][p + 1, 8:40, :] = plane
-            acc = pack_fine(plane, k, p, acc)
-        s["PZ"][k] = acc
-    pl.semaphore_wait(barrier, len(SIX))
-
-    cc = send_fine(c_ref.at[0], c_ref.at[15], 0)
-    vv = send_fine(v_ref.at[0], v_ref.at[15], 1)
-    restrict_fine(lambda p: c_ref[p], "c")
+    restrict_fine(lambda p: s["C0"][p + 1, 8:40, :], "c")
     restrict_one(lambda p: s["B1c"][p], 0, "c")
-    take_fine(s["C0"], 0, cc)
+    arrive(copies)
+    take_fine("C0", 0)
     weights("0", 16, 32, 1.0, fine_z(0))
-    take_fine(s["V0"], 1, vv)
+    take_fine("V0", 1)
 
     def sweep_fine(src, dst, zs, k):
         acc = jnp.zeros((32, 128), F32)
@@ -387,13 +431,15 @@
             s[dst][p + 1, 8:40, :] = new
             acc = pack_fine(new, k, p, acc)
         s["PZ"][k] = acc
-        return send_fine(s[dst].at[1, 8:40], s[dst].at[16, 8:40], k)
+        return send_fine((dst,), k)
 
     copies = sweep_fine("V0", "V1", fine_z(1), 2)
-    take_fine(s["V1"], 2, copies)
+    arrive(copies)
+    take_fine("V1", 2)
     copies = sweep_fine("V1", "X0", fine_z(2), 3)
     c_one = send_one("c", 5)
-    take_fine(s["X0"], 3, copies)
+    arrive(copies)
+    take_fine("X0", 3)
     restrict_fine(lambda p: residual("0", s["X0"], p, 32, g_ref[p], fine_z(3)), "g")
 
     g_one = send_one("g", 4)
@@ -422,20 +468,20 @@
     g_two = send_two("g")
     take_two(s["C2"], "c", c_two)
     restrict_two(lambda p: s["C2"][p + 1, 16:24, :], "c")
-    c_z = send_z("c")
+    c_core = send_core("c")
     weights("2", 16, 24, 0.0625, plain_z)
+    c_chips = send_chips("c", c_core)
     take_two(s["G2"], "g", g_two)
     begin("2")
     sweep("2", "EA2", "EB2")
     rest2 = left("2", "EB2")
     restrict_two(lambda p: rest2(p)[8:16], "g")
 
-    g_z = send_z("g")
-    c_y = pass_y("c", c_z)
-    g_y = pass_y("g", g_z)
-    arrive(c_y)
-    for g in range(NY):
-        s["C3"][1:9, 8 + 4 * g : 12 + 4 * g, :] = s["S4c"][g]
+    for i, value in enumerate(constants()[0]):
+        s["K"][i] = F32(value)
+    g_core = send_core("g")
+    g_chips = send_chips("g", g_core)
+    take_coarse(s["C3"], 1, 8, "c", c_chips)
     weights("3", 8, 32, 0.015625, closed_z)
     at = lane((32, 128))
     for p in range(8):
@@ -447,9 +493,7 @@
         s["WYP3"][p] = s["WY3"][p, 1:33] * inv
         s["WZM3"][p] = jnp.where(at == 0, 0.0, s["WZM3"][p] * inv)
         s["WZP3"][p] = jnp.where(at == 127, 0.0, s["WZP3"][p] * inv)
-    arrive(g_y)
-    for g in range(NY):
-        s["T3"][:, 4 * g : 4 * g + 4, :] = s["S4g"][g]
+    take_coarse(s["T3"], 0, 0, "g", g_chips)
     theta = constants()[1]
     for p in range(8):
         t = s["T3"][p] * s["SD3"][p]
@@ -459,7 +503,7 @@
         s["KA"][p + 1, 8:40, :] = d
 
     def cheb(src, dst, i):
-        a, b = k_ref[2 * i], k_ref[2 * i + 1]
+        a, b = s["K"][2 * i], s["K"][2 * i + 1]
         v = s[src]
         for p in range(8):
             e = v[p + 1, 8:40, :]
@@ -519,26 +563,33 @@
             s["VP"][i, 7:8, :] = s["X0"][i, 7:8, :] + s["TA"][j, 3:4, :]
             s["VP"][i, 40:41, :] = s["X0"][i, 40:41, :] + s["TA"][j, 20:21, :]
     copies = sweep_fine("VP", "VQ", fine_z(3, lambda p: s["DB"][(p + 2) // 2]), 4)
-    take_fine(s["VQ"], 4, copies)
+    arrive(copies)
+    take_fine("VQ", 4)
+    stores = []
     for p in range(16):
-        o_ref[p] = swept("0", s["VQ"], p, 32, g_ref[p], fine_z(4))
-    for copy in started:
-        copy.wait_send()
+        s["OV"][p] = swept("0", s["VQ"], p, 32, g_ref[p], fine_z(4))
+        if p % 4 == 3:
+            part = pl.ds(p - 3, 4)
+            stores.append(pltpu.make_async_copy(s["OV"].at[part], o_ref.at[part], s["hs"].at[3 + p // 4]))
+            stores[-1].start()
+    for copy, cond in started:
+        when(cond, copy.wait_send)
+    for copy in stores:
+        copy.wait()
 
 
 def on_device(right_side, coefficient, guess):
-    table = jnp.asarray(constants()[0])
-    vmem = pl.BlockSpec(memory_space=pltpu.VMEM)
+    whole = pl.BlockSpec(memory_space=pl.ANY)
     return pl.pallas_call(
         kernel,
         out_shape=jax.ShapeDtypeStruct((16, 32, 128), F32),
-        in_specs=[pl.BlockSpec(memory_space=pltpu.SMEM), vmem, vmem, vmem],
-        out_specs=vmem,
+        in_specs=[whole, whole, whole],
+        out_specs=whole,
         scratch_shapes=[build_scratch()],
         compiler_params=pltpu.CompilerParams(
             collective_id=0, has_side_effects=True, vmem_limit_bytes=56 * 2**20
         ),
-    )(table, right_side, coefficient, guess)
+    )(right_side, coefficient, guess)
 
 
 def solution(mesh):

time: 56.5 us -> 54.7 us (0.968)
  Pallas kernels: 54.6 us -> 52.9 us
    pallas_call x1, Pallas kernels: 54.6 us -> 52.9 us  [on_device(): pl.pallas_call(kernel, out_shape=jax.ShapeDtypeStruct((16, 32, 128), F32)...]
where the time goes in v2:
time: 54.7 us; the launch traced here: 54.6 us
  Pallas kernels  52.9 us (97%)
  local copies, waits for them, and re-layouts  1.67 us (3%)
    pallas_call x1, Pallas kernels, on_device(): pl.pallas_call(kernel, out_shape=jax.ShapeDtypeStruct((16, 32, 128), F32)...  52.9 us
    unnamed x1, local copies, waits for them, and re-layouts  1.67 us

profile of v2, /device:TPU:1, one launch (start us, length us, event | category | flops | bytes accessed | tf_op | source)
XLA Modules:
  0.0 54.6 jit_solution(15656137553859673217)
XLA Ops:
  0.0 52.9 %shard_map.37 = f32[16,32,128]{2,1,0:T(8,128)} custom-call(f32[16,32,128]{2,1,0:T(8,128)} %g_hbm.1, f32[16,32,128]{2,1,0:T(8,128)} %c_hbm.1, f32[16,32,128]{2,1,0:T(8,128)} %v_hbm.1), custom_call_target="tpu_custom_call" | custom-call | tf_op jit(solution)/shard_map/pallas_call | solution.py:583
  52.9 1.7 %copy.5 = f32[16,32,128]{2,1,0:T(8,128)} copy(f32[16,32,128]{2,1,0:T(8,128)} %shard_map.37) | data formatting | bytes 524288

commit v3 on v2

--- a/solution.py
+++ b/solution.py
@@ -28,9 +28,6 @@
     (o for o in itertools.product((0,), range(NY), range(0, NZ, 2)) if o != (0, 0, 0)),
     key=lambda o: -(min(o[1], NY - o[1]) + min(o[2], NZ - o[2]) // 2),
 )
-NEAR = {(o[0], o[1] % NY, o[2] % NZ) for o in SIX}
-FAR = [o for o in CHIPS if o not in NEAR]
-
 
 def side(d):
     return 0 if d < 0 else 1
@@ -112,6 +109,7 @@
         s.update({"WX" + l: vm(17, 24, 128), "WY" + l: vm(16, 32, 128)})
         for name in ("WZM", "WZP", "D", "SD"):
             s[name + l] = vm(16, 24, 128)
+    s["wrap"] = pltpu.SemaphoreType.REGULAR((3, 3))
     s["K"] = pltpu.SMEM((2 * (CHEB - 1),), F32)
     s.update(U2=vm(20, 24, 128), T21=vm(8, 24, 128), D21=vm(8, 24, 128))
     s.update(TA=vm(10, 24, 128), TB=vm(10, 24, 128), DA=vm(10, 48, 128), DB=vm(10, 32, 128))
@@ -162,6 +160,21 @@
         when(out, copy.start)
         started.append((copy, out))
         return copy, exists(tuple(-d for d in o), axes)
+
+    def edges(o):
+        axis = next(i for i in range(3) if o[i])
+        return jnp.logical_not(here[axis][o[axis]]), s["wrap"], axis
+
+    def tell_edges(k):
+        for o in SIX:
+            cond, sem, axis = edges(o)
+            when(cond, lambda: pl.semaphore_signal(
+                sem.at[k, axis], inc=1, device_id=target(o), device_id_type=MESH))
+
+    def hear_edges(k):
+        for o in SIX:
+            cond, sem, axis = edges(o)
+            when(cond, lambda: pl.semaphore_wait(sem.at[k, axis], 1))
 
     def arrive(copies):
         for copy, cond in copies:
@@ -178,8 +191,6 @@
     ]
     for load in loads:
         load.start()
-    for o in FAR:
-        pl.semaphore_signal(barrier, inc=1, device_id=target(o), device_id_type=MESH)
 
     def pack_fine(plane, k, p, acc):
         s["YB"][0, k, p] = plane[0:1]
@@ -303,7 +314,7 @@
             qs[q, 4:8] = half[2 * q + 1]
         s["PB3" + k][...] = sum(mm(qs[q], to_three[q]) for q in range(4))
 
-    def send_one(k, h):
+    def send_one(k, h, axes=(0, 1, 2)):
         out = []
         b, pz = s["B1" + k], s["PZ1" + k]
         for i, (dx, dy, dz) in enumerate(AROUND):
@@ -318,7 +329,7 @@
                     src, dst = b.at[xs], s["RX1" + k].at[side(-dx)]
                 else:
                     src, dst = b.at[:, ys], s["RY1" + k].at[side(-dy)]
-            out.append(send(src, dst, s["ss1" + k].at[i], s["rs1" + k].at[i], (dx, dy, dz)))
+            out.append(send(src, dst, s["ss1" + k].at[i], s["rs1" + k].at[i], (dx, dy, dz), axes))
         return out
 
     def take_one(e, k, h, copies):
@@ -352,11 +363,11 @@
                 moved = roll(zs[1 + dx, lo:hi], 16 - 16 * (start + i))
                 e[base + i, lo:hi, :] = jnp.where(halo, moved, e[base + i, lo:hi, :])
 
-    def send_two(k):
+    def send_two(k, axes=(1, 2)):
         out = []
         for i, (a, dy, dz) in enumerate(WIDE):
             dst = s["S2" + k].at[gx, 1 - dy, 1 - dz]
-            out.append(send(s["PB2" + k], dst, s["ss2" + k].at[i], s["rs2" + k].at[i], (a, dy, dz), (1, 2)))
+            out.append(send(s["PB2" + k], dst, s["ss2" + k].at[i], s["rs2" + k].at[i], (a, dy, dz), axes))
         s["S2" + k][gx, 1, 1] = s["PB2" + k][...]
         return out
 
@@ -404,9 +415,10 @@
         for p in range(16):
             acc = pack_fine(s[name][p + 1, 8:40, :], k, p, acc)
         s["PZ"][k] = acc
-    pl.semaphore_wait(barrier, len(SIX) + len(FAR))
+    pl.semaphore_wait(barrier, len(SIX))
 
     copies = send_fine(("C0", "V0"), 0)
+    tell_edges(0)
     loads[2].wait()
     g_ref = s["GV"]
     for name in ("C1", "G1", "EA1", "EB1", "C2", "G2", "EA2", "EB2"):
@@ -420,6 +432,7 @@
     restrict_fine(lambda p: s["C0"][p + 1, 8:40, :], "c")
     restrict_one(lambda p: s["B1c"][p], 0, "c")
     arrive(copies)
+    hear_edges(0)
     take_fine("C0", 0)
     weights("0", 16, 32, 1.0, fine_z(0))
     take_fine("V0", 1)
@@ -434,17 +447,21 @@
         return send_fine((dst,), k)
 
     copies = sweep_fine("V0", "V1", fine_z(1), 2)
+    tell_edges(1)
     arrive(copies)
+    hear_edges(1)
     take_fine("V1", 2)
     copies = sweep_fine("V1", "X0", fine_z(2), 3)
-    c_one = send_one("c", 5)
+    tell_edges(2)
+    c_one = send_one("c", 5, ())
     arrive(copies)
+    hear_edges(2)
     take_fine("X0", 3)
     restrict_fine(lambda p: residual("0", s["X0"], p, 32, g_ref[p], fine_z(3)), "g")
 
     g_one = send_one("g", 4)
     take_one(s["C1"], "c", 5, c_one)
-    c_two = send_two("c")
+    c_two = send_two("c", ())
     weights("1", 16, 24, 0.25, plain_z)
     take_one(s["G1"], "g", 4, g_one)
 

time: 54.7 us -> 52.6 us (0.962)
  Pallas kernels: 52.9 us -> 50.8 us
    pallas_call x1, Pallas kernels: 52.9 us -> 50.8 us  [on_device(): pl.pallas_call(kernel, out_shape=jax.ShapeDtypeStruct((16, 32, 128), F32)...]
where the time goes in v3:
time: 52.6 us; the launch traced here: 52.5 us
  Pallas kernels  50.8 us (97%)
  local copies, waits for them, and re-layouts  1.67 us (3%)
    pallas_call x1, Pallas kernels, on_device(): pl.pallas_call(kernel, out_shape=jax.ShapeDtypeStruct((16, 32, 128), F32)...  50.8 us
    unnamed x1, local copies, waits for them, and re-layouts  1.67 us

profile of v3, /device:TPU:1, one launch (start us, length us, event | category | flops | bytes accessed | tf_op | source)
XLA Modules:
  0.0 52.5 jit_solution(2969409404498202055)
XLA Ops:
  0.0 50.8 %shard_map.37 = f32[16,32,128]{2,1,0:T(8,128)} custom-call(f32[16,32,128]{2,1,0:T(8,128)} %g_hbm.1, f32[16,32,128]{2,1,0:T(8,128)} %c_hbm.1, f32[16,32,128]{2,1,0:T(8,128)} %v_hbm.1), custom_call_target="tpu_custom_call" | custom-call | tf_op jit(solution)/shard_map/pallas_call | solution.py:600
  50.8 1.7 %copy.5 = f32[16,32,128]{2,1,0:T(8,128)} copy(f32[16,32,128]{2,1,0:T(8,128)} %shard_map.37) | data formatting | bytes 524288

commit v4 on v3

--- a/solution.py
+++ b/solution.py
@@ -82,7 +82,7 @@
     s.update(
         YB=vm(2, 5, 16, 1, 128), PZ=vm(5, 32, 128),
         RX=vm(5, 2, 32, 128), RY=vm(2, 5, 16, 1, 128), RZ=vm(2, 5, 32, 128), MZ=vm(5, 32, 128),
-        ss0=dma(5, 6), rs0=dma(5, 6), hs=dma(8), GV=vm(16, 32, 128), OV=vm(16, 32, 128),
+        ss=dma(65), rs=dma(65), W=vm(92, 8, 128), hs=dma(8), GV=vm(16, 32, 128), OV=vm(16, 32, 128),
     )
     s.update(RS0=vm(8, 32, 128), RS1=vm(4, 24, 128), RS2=vm(8, 8, 128), QS=vm(4, 8, 128))
     for k, h in (("c", 5), ("g", 4)):
@@ -92,24 +92,20 @@
         s["RY1" + k] = vm(2, 8, 8, 128)
         s["RE1" + k] = vm(2, 2, h, 8, 128)
         s["RZ1" + k] = vm(2, 3, 3, 16, 128)
-        s["ss1" + k], s["rs1" + k] = dma(26), dma(26)
         s["ZS" + k] = vm(3, 40, 128)
         s["PB2" + k] = vm(8, 128)
         s["S2" + k] = vm(NX, 3, 3, 8, 128)
-        s["ss2" + k], s["rs2" + k] = dma(len(WIDE)), dma(len(WIDE))
         s["PB3" + k] = vm(8, 128)
         s["S3" + k] = vm(8, 128)
         s["YS" + k] = vm(8, 128)
         s["S4" + k] = vm(NY, NZ // 2, 8, 128)
-        s["ss3" + k], s["rs3" + k] = dma(1), dma(1)
-        s["ss4" + k], s["rs4" + k] = dma(len(CHIPS)), dma(len(CHIPS))
     for l in ("1", "2"):
         for name in ("C", "G", "EA", "EB"):
             s[name + l] = vm(18, 40, 128)
         s.update({"WX" + l: vm(17, 24, 128), "WY" + l: vm(16, 32, 128)})
         for name in ("WZM", "WZP", "D", "SD"):
             s[name + l] = vm(16, 24, 128)
-    s["wrap"] = pltpu.SemaphoreType.REGULAR((3, 3))
+    s["wrap"] = pltpu.SemaphoreType.REGULAR((3,))
     s["K"] = pltpu.SMEM((2 * (CHEB - 1),), F32)
     s.update(U2=vm(20, 24, 128), T21=vm(8, 24, 128), D21=vm(8, 24, 128))
     s.update(TA=vm(10, 24, 128), TB=vm(10, 24, 128), DA=vm(10, 48, 128), DB=vm(10, 32, 128))
@@ -129,7 +125,7 @@
         2: {-1: gz > 0, 1: gz < NZ - 1},
     }
     core = lax.rem(gz, 2)
-    started = []
+    started, taken = [], {}
 
     def exists(o, axes=(0, 1, 2)):
         cond = None
@@ -151,30 +147,47 @@
     def target(o):
         return (lax.rem(gx + o[0] + NX, NX), lax.rem(gy + o[1] + NY, NY), lax.rem(gz + o[2] + NZ, NZ))
 
-    def send(src, dst, ss, rs, o, axes=(0, 1, 2), to=None):
+    def send(src, dst, group, o, axes=(0, 1, 2), to=None):
+        at = taken.setdefault(group, len(taken))
         copy = pltpu.make_async_remote_copy(
-            src_ref=src, dst_ref=dst, send_sem=ss, recv_sem=rs,
+            src_ref=src, dst_ref=dst, send_sem=s["ss"].at[at], recv_sem=s["rs"].at[at],
             device_id=target(o) if to is None else to, device_id_type=MESH,
         )
         out = exists(o, axes)
         when(out, copy.start)
-        started.append((copy, out))
-        return copy, exists(tuple(-d for d in o), axes)
+        return group, copy, out, exists(tuple(-d for d in o), axes), int(np.prod(src.shape)) // 1024
+
+    def grouped(copies):
+        groups = {}
+        for group, copy, out, back, tiles in copies:
+            groups.setdefault(group, []).append((copy, out, back, tiles))
+        waits = []
+        for group, members in groups.items():
+            copy, out, back, tiles = members[0]
+            if len(members) > 1:
+                at, part = taken[group], s["W"].at[pl.ds(0, sum(m[3] for m in members))]
+                copy = pltpu.make_async_remote_copy(
+                    src_ref=part, dst_ref=part, send_sem=s["ss"].at[at], recv_sem=s["rs"].at[at],
+                    device_id=target((0, 0, 1)), device_id_type=MESH,
+                )
+            started.append((copy, out))
+            waits.append((copy, back))
+        return waits
 
     def edges(o):
         axis = next(i for i in range(3) if o[i])
         return jnp.logical_not(here[axis][o[axis]]), s["wrap"], axis
 
-    def tell_edges(k):
+    def tell_edges():
         for o in SIX:
             cond, sem, axis = edges(o)
             when(cond, lambda: pl.semaphore_signal(
-                sem.at[k, axis], inc=1, device_id=target(o), device_id_type=MESH))
-
-    def hear_edges(k):
+                sem.at[axis], inc=1, device_id=target(o), device_id_type=MESH))
+
+    def hear_edges():
         for o in SIX:
             cond, sem, axis = edges(o)
-            when(cond, lambda: pl.semaphore_wait(sem.at[k, axis], 1))
+            when(cond, lambda: pl.semaphore_wait(sem.at[axis], 1))
 
     def arrive(copies):
         for copy, cond in copies:
@@ -201,18 +214,17 @@
 
     def send_fine(names, k):
         out = []
-        ss, rs = s["ss0"], s["rs0"]
         yb, rx, ry, rz, pz = s["YB"], s["RX"], s["RY"], s["RZ"], s["PZ"]
         ks = pl.ds(k, len(names))
-        out.append(send(yb.at[1, ks], ry.at[0, ks], ss.at[k, 0], rs.at[k, 0], (0, 1, 0)))
-        out.append(send(yb.at[0, ks], ry.at[1, ks], ss.at[k, 1], rs.at[k, 1], (0, -1, 0)))
+        out.append(send(yb.at[1, ks], ry.at[0, ks], (k, 0), (0, 1, 0)))
+        out.append(send(yb.at[0, ks], ry.at[1, ks], (k, 1), (0, -1, 0)))
         for i, name in enumerate(names):
             low, high = s[name].at[1, pl.ds(8, 32)], s[name].at[16, pl.ds(8, 32)]
-            out.append(send(high, rx.at[k + i, 0], ss.at[k + i, 2], rs.at[k + i, 2], (1, 0, 0)))
-            out.append(send(low, rx.at[k + i, 1], ss.at[k + i, 3], rs.at[k + i, 3], (-1, 0, 0)))
-        out.append(send(pz.at[ks], rz.at[0, ks], ss.at[k, 4], rs.at[k, 4], (0, 0, 1)))
-        out.append(send(pz.at[ks], rz.at[1, ks], ss.at[k, 5], rs.at[k, 5], (0, 0, -1)))
-        return out
+            out.append(send(high, rx.at[k + i, 0], (k, 2), (1, 0, 0)))
+            out.append(send(low, rx.at[k + i, 1], (k, 3), (-1, 0, 0)))
+        out.append(send(pz.at[ks], rz.at[0, ks], (k, 4), (0, 0, 1)))
+        out.append(send(pz.at[ks], rz.at[1, ks], (k, 5), (0, 0, -1)))
+        return grouped(out)
 
     def take_fine(name, k):
         v = s[name]
@@ -329,8 +341,8 @@
                     src, dst = b.at[xs], s["RX1" + k].at[side(-dx)]
                 else:
                     src, dst = b.at[:, ys], s["RY1" + k].at[side(-dy)]
-            out.append(send(src, dst, s["ss1" + k].at[i], s["rs1" + k].at[i], (dx, dy, dz), axes))
-        return out
+            out.append(send(src, dst, ("one", k, i if axes else 0), (dx, dy, dz), axes))
+        return grouped(out)
 
     def take_one(e, k, h, copies):
         arrive(copies)
@@ -367,9 +379,9 @@
         out = []
         for i, (a, dy, dz) in enumerate(WIDE):
             dst = s["S2" + k].at[gx, 1 - dy, 1 - dz]
-            out.append(send(s["PB2" + k], dst, s["ss2" + k].at[i], s["rs2" + k].at[i], (a, dy, dz), axes))
+            out.append(send(s["PB2" + k], dst, ("two", k, (dy, dz) if axes else 0), (a, dy, dz), axes))
         s["S2" + k][gx, 1, 1] = s["PB2" + k][...]
-        return out
+        return grouped(out)
 
     def take_two(e, k, copies):
         arrive(copies)
@@ -385,7 +397,7 @@
 
     def send_core(k):
         to = (gx, gy, gz + 1 - 2 * core)
-        return [send(s["PB3" + k], s["S3" + k], s["ss3" + k].at[0], s["rs3" + k].at[0], (0, 0, 0), to=to)]
+        return grouped([send(s["PB3" + k], s["S3" + k], ("core", k), (0, 0, 0), to=to)])
 
     def send_chips(k, copies):
         arrive(copies)
@@ -393,9 +405,9 @@
         out = []
         for i, o in enumerate(CHIPS):
             dst = s["S4" + k].at[gy, gz // 2]
-            out.append(send(s["YS" + k], dst, s["ss4" + k].at[i], s["rs4" + k].at[i], o, ()))
+            out.append(send(s["YS" + k], dst, ("chips", k), o, ()))
         s["S4" + k][gy, gz // 2] = s["YS" + k][...]
-        return out
+        return grouped(out)
 
     def take_coarse(dst, base, row, k, copies):
         arrive(copies)
@@ -418,7 +430,7 @@
     pl.semaphore_wait(barrier, len(SIX))
 
     copies = send_fine(("C0", "V0"), 0)
-    tell_edges(0)
+    tell_edges()
     loads[2].wait()
     g_ref = s["GV"]
     for name in ("C1", "G1", "EA1", "EB1", "C2", "G2", "EA2", "EB2"):
@@ -432,7 +444,7 @@
     restrict_fine(lambda p: s["C0"][p + 1, 8:40, :], "c")
     restrict_one(lambda p: s["B1c"][p], 0, "c")
     arrive(copies)
-    hear_edges(0)
+    hear_edges()
     take_fine("C0", 0)
     weights("0", 16, 32, 1.0, fine_z(0))
     take_fine("V0", 1)
@@ -447,15 +459,15 @@
         return send_fine((dst,), k)
 
     copies = sweep_fine("V0", "V1", fine_z(1), 2)
-    tell_edges(1)
+    tell_edges()
     arrive(copies)
-    hear_edges(1)
+    hear_edges()
     take_fine("V1", 2)
     copies = sweep_fine("V1", "X0", fine_z(2), 3)
-    tell_edges(2)
+    tell_edges()
     c_one = send_one("c", 5, ())
     arrive(copies)
-    hear_edges(2)
+    hear_edges()
     take_fine("X0", 3)
     restrict_fine(lambda p: residual("0", s["X0"], p, 32, g_ref[p], fine_z(3)), "g")
 

time: 52.6 us -> 49.7 us (0.945)
  Pallas kernels: 50.8 us -> 47.9 us
    pallas_call x1, Pallas kernels: 50.8 us -> 47.9 us  [on_device(): pl.pallas_call(kernel, out_shape=jax.ShapeDtypeStruct((16, 32, 128), F32)...]
where the time goes in v4:
time: 49.7 us; the launch traced here: 49.6 us
  Pallas kernels  47.9 us (96%)
  local copies, waits for them, and re-layouts  1.67 us (3%)
    pallas_call x1, Pallas kernels, on_device(): pl.pallas_call(kernel, out_shape=jax.ShapeDtypeStruct((16, 32, 128), F32)...  47.9 us
    unnamed x1, local copies, waits for them, and re-layouts  1.67 us

profile of v4, /device:TPU:1, one launch (start us, length us, event | category | flops | bytes accessed | tf_op | source)
XLA Modules:
  0.0 49.6 jit_solution(4204553495758864880)
XLA Ops:
  0.0 47.9 %shard_map.37 = f32[16,32,128]{2,1,0:T(8,128)} custom-call(f32[16,32,128]{2,1,0:T(8,128)} %g_hbm.1, f32[16,32,128]{2,1,0:T(8,128)} %c_hbm.1, f32[16,32,128]{2,1,0:T(8,128)} %v_hbm.1), custom_call_target="tpu_custom_call" | custom-call | tf_op jit(solution)/shard_map/pallas_call | solution.py:612
  47.9 1.7 %copy.5 = f32[16,32,128]{2,1,0:T(8,128)} copy(f32[16,32,128]{2,1,0:T(8,128)} %shard_map.37) | data formatting | bytes 524288

commit v5 on v4

--- a/solution.py
+++ b/solution.py
@@ -53,15 +53,20 @@
 
 
 def mm(x, m):
-    return lax.dot_general(
-        x, m, (((1,), (0,)), ((), ())), precision=lax.Precision.HIGHEST, preferred_element_type=F32
-    )
+    rows = x.shape[0]
+    high = x.astype(jnp.bfloat16)
+    rest = x - high.astype(F32)
+    mid = rest.astype(jnp.bfloat16)
+    low = (rest - mid.astype(F32)).astype(jnp.bfloat16)
+    terms = jnp.concatenate([high, mid, low], axis=0)
+    out = lax.dot_general(terms, m, (((1,), (0,)), ((), ())), preferred_element_type=F32)
+    return out[0:rows] + out[rows : 2 * rows] + out[2 * rows :]
 
 
 def picks(condition, width=128, value=1.0):
     row = lax.broadcasted_iota(jnp.int32, (128, width), 0)
     col = lax.broadcasted_iota(jnp.int32, (128, width), 1)
-    return jnp.where(condition(row, col), F32(value), F32(0.0))
+    return jnp.where(condition(row, col), F32(value), F32(0.0)).astype(jnp.bfloat16)
 
 
 def vm(*shape):
@@ -82,7 +87,7 @@
     s.update(
         YB=vm(2, 5, 16, 1, 128), PZ=vm(5, 32, 128),
         RX=vm(5, 2, 32, 128), RY=vm(2, 5, 16, 1, 128), RZ=vm(2, 5, 32, 128), MZ=vm(5, 32, 128),
-        ss=dma(65), rs=dma(65), W=vm(92, 8, 128), hs=dma(8), GV=vm(16, 32, 128), OV=vm(16, 32, 128),
+        ss=dma(42), rs=dma(42), W=vm(92, 8, 128), hs=dma(8), GV=vm(16, 32, 128), OV=vm(16, 32, 128),
     )
     s.update(RS0=vm(8, 32, 128), RS1=vm(4, 24, 128), RS2=vm(8, 8, 128), QS=vm(4, 8, 128))
     for k, h in (("c", 5), ("g", 4)):
@@ -267,32 +272,32 @@
             s["WZM" + l][p], s["WZP" + l][p], s["D" + l][p] = wzm, wzp, d
             s["SD" + l][p] = jnp.where(mid > 0, F32(OMEGA) / d, 0.0)
 
-    def gathered(l, v, p, rows, right, zs):
+    def gathered(l, v, p, rows, right, zs, skip=0):
         wx, wy = s["WX" + l], s["WY" + l]
-        mid = v[p + 1, 8 : 8 + rows, :]
+        lo, hi, up, here_ = 8 + skip, 8 + skip + rows, slice(skip + 1, skip + rows + 1), slice(skip, skip + rows)
+        mid = v[p + 1, lo:hi, :]
         zm, zp = zs(p, mid)
-        total = right + wx[p] * v[p, 8 : 8 + rows, :] + wx[p + 1] * v[p + 2, 8 : 8 + rows, :]
-        total = total + wy[p, 0:rows] * v[p + 1, 7 : 7 + rows, :]
-        total = total + wy[p, 1 : rows + 1] * v[p + 1, 9 : 9 + rows, :]
-        total = total + s["WZM" + l][p] * zm + s["WZP" + l][p] * zp
+        total = right + wx[p, here_] * v[p, lo:hi, :] + wx[p + 1, here_] * v[p + 2, lo:hi, :]
+        total = total + wy[p, here_] * v[p + 1, lo - 1 : hi - 1, :]
+        total = total + wy[p, up] * v[p + 1, lo + 1 : hi + 1, :]
+        total = total + s["WZM" + l][p, here_] * zm + s["WZP" + l][p, here_] * zp
         return mid, total
 
     def swept(l, v, p, rows, right, zs):
         mid, total = gathered(l, v, p, rows, right, zs)
         return mid * F32(1.0 - OMEGA) + s["SD" + l][p] * total
 
-    def residual(l, v, p, rows, right, zs):
-        mid, total = gathered(l, v, p, rows, right, zs)
-        return total - s["D" + l][p] * mid
+    def residual(l, v, p, rows, right, zs, skip=0):
+        mid, total = gathered(l, v, p, rows, right, zs, skip)
+        return total - s["D" + l][p, skip : skip + rows] * mid
 
     to_one = picks(lambda r, c: r // 2 + 32 == c, value=0.125)
-    to_two = [
-        picks(lambda r, c, p=p: (c // 32 == p) & (r // 2 == c % 32 + 16), value=0.125) for p in range(4)
-    ]
-    to_three = [
-        picks(lambda r, c, q=q: (c // 16 == 2 * q + core) & (r // 2 == c % 16 + 16), value=0.125)
-        for q in range(4)
-    ]
+    to_two = picks(lambda r, c: (c < 32) & (r // 2 == c + 16), value=0.125)
+    to_three = picks(lambda r, c: (c // 16 == core) & (r // 2 == c % 16 + 16), value=0.125)
+
+    def side_by_side(x, m):
+        out = mm(x.reshape(32, 128), m)
+        return out[0:8] + roll(out[8:16], 32) + roll(out[16:24], 64) + roll(out[24:32], 96)
 
     def restrict_fine(plane, k):
         rs = s["RS0"]
@@ -314,7 +319,7 @@
         for q in range(4):
             rs[q, 0:rows] = plane(2 * q) + plane(2 * q + 1)
         half = rs[:, pl.ds(first, 8, stride=2), :] + rs[:, pl.ds(first + 1, 8, stride=2), :]
-        s["PB2" + k][...] = sum(mm(half[p], to_two[p]) for p in range(4))
+        s["PB2" + k][...] = side_by_side(half, to_two)
 
     def restrict_two(plane, k):
         rs, qs = s["RS2"], s["QS"]
@@ -324,9 +329,9 @@
         for q in range(4):
             qs[q, 0:4] = half[2 * q]
             qs[q, 4:8] = half[2 * q + 1]
-        s["PB3" + k][...] = sum(mm(qs[q], to_three[q]) for q in range(4))
-
-    def send_one(k, h, axes=(0, 1, 2)):
+        s["PB3" + k][...] = side_by_side(qs[...], to_three)
+
+    def send_one(k, h, axes=(0, 1)):
         out = []
         b, pz = s["B1" + k], s["PZ1" + k]
         for i, (dx, dy, dz) in enumerate(AROUND):
@@ -341,7 +346,7 @@
                     src, dst = b.at[xs], s["RX1" + k].at[side(-dx)]
                 else:
                     src, dst = b.at[:, ys], s["RY1" + k].at[side(-dy)]
-            out.append(send(src, dst, ("one", k, i if axes else 0), (dx, dy, dz), axes))
+            out.append(send(src, dst, ("one", k, (dx, dy) if axes else 0), (dx, dy, dz), axes))
         return grouped(out)
 
     def take_one(e, k, h, copies):
@@ -375,11 +380,11 @@
                 moved = roll(zs[1 + dx, lo:hi], 16 - 16 * (start + i))
                 e[base + i, lo:hi, :] = jnp.where(halo, moved, e[base + i, lo:hi, :])
 
-    def send_two(k, axes=(1, 2)):
+    def send_two(k, axes=(1,)):
         out = []
         for i, (a, dy, dz) in enumerate(WIDE):
             dst = s["S2" + k].at[gx, 1 - dy, 1 - dz]
-            out.append(send(s["PB2" + k], dst, ("two", k, (dy, dz) if axes else 0), (a, dy, dz), axes))
+            out.append(send(s["PB2" + k], dst, ("two", k, dy if axes else 0), (a, dy, dz), axes))
         s["S2" + k][gx, 1, 1] = s["PB2" + k][...]
         return grouped(out)
 
@@ -477,12 +482,12 @@
     weights("1", 16, 24, 0.25, plain_z)
     take_one(s["G1"], "g", 4, g_one)
 
-    def begin(l):
-        for p in range(16):
+    def begin(l, planes=range(16)):
+        for p in planes:
             s["EA" + l][p + 1, 8:32, :] = s["SD" + l][p] * s["G" + l][p + 1, 8:32, :]
 
-    def sweep(l, src, dst):
-        for p in range(16):
+    def sweep(l, src, dst, planes=range(16)):
+        for p in planes:
             right = s["G" + l][p + 1, 8:32, :]
             s[dst][p + 1, 8:32, :] = swept(l, s[src], p, 24, right, plain_z)
 
@@ -490,7 +495,7 @@
         return lambda p: residual(l, s[src], p, 24, s["G" + l][p + 1, 8:32, :], plain_z)
 
     begin("1")
-    sweep("1", "EA1", "EB1")
+    sweep("1", "EA1", "EB1", range(1, 15))
     rest = left("1", "EB1")
     restrict_one(lambda p: rest(p + 4), 4, "g")
 
@@ -503,8 +508,7 @@
     take_two(s["G2"], "g", g_two)
     begin("2")
     sweep("2", "EA2", "EB2")
-    rest2 = left("2", "EB2")
-    restrict_two(lambda p: rest2(p)[8:16], "g")
+    restrict_two(lambda p: residual("2", s["EB2"], p, 8, s["G2"][p + 1, 16:24, :], plain_z, 8), "g")
 
     for i, value in enumerate(constants()[0]):
         s["K"][i] = F32(value)
@@ -571,10 +575,10 @@
     s["T21"][...] = mm(part.reshape(192, 128), from_two).reshape(8, 24, 128)
     for o in (0, 1):
         s["D21"][:, pl.ds(o, 12, stride=2), :] = s["T21"][:, 6:18, :]
-    for p in range(16):
+    for p in range(1, 15):
         s["EA1"][p + 1, 8:32, :] = s["EB1"][p + 1, 8:32, :] + s["D21"][p // 2]
-    sweep("1", "EA1", "EB1")
-    sweep("1", "EB1", "EA1")
+    sweep("1", "EA1", "EB1", range(2, 14))
+    sweep("1", "EB1", "EA1", range(3, 13))
 
     from_one = picks(
         lambda r, c: ((c < 128) & (r == 32 + c // 2)) | ((c == 128) & (r == 31)) | ((c == 255) & (r == 96)), 256
@@ -591,7 +595,10 @@
         if 0 < i < 17:
             s["VP"][i, 7:8, :] = s["X0"][i, 7:8, :] + s["TA"][j, 3:4, :]
             s["VP"][i, 40:41, :] = s["X0"][i, 40:41, :] + s["TA"][j, 20:21, :]
+    earlier = len(started)
     copies = sweep_fine("VP", "VQ", fine_z(3, lambda p: s["DB"][(p + 2) // 2]), 4)
+    for copy, cond in started[:earlier]:
+        when(cond, copy.wait_send)
     arrive(copies)
     take_fine("VQ", 4)
     stores = []
@@ -601,7 +608,7 @@
             part = pl.ds(p - 3, 4)
             stores.append(pltpu.make_async_copy(s["OV"].at[part], o_ref.at[part], s["hs"].at[3 + p // 4]))
             stores[-1].start()
-    for copy, cond in started:
+    for copy, cond in started[earlier:]:
         when(cond, copy.wait_send)
     for copy in stores:
         copy.wait()

time: 49.7 us -> 48.7 us (0.980)
  Pallas kernels: 47.9 us -> 46.9 us
    pallas_call x1, Pallas kernels: 47.9 us -> 46.9 us  [on_device(): pl.pallas_call(kernel, out_shape=jax.ShapeDtypeStruct((16, 32, 128), F32)...]
where the time goes in v5:
time: 48.7 us; the launch traced here: 48.6 us
  Pallas kernels  46.9 us (96%)
  local copies, waits for them, and re-layouts  1.67 us (3%)
    pallas_call x1, Pallas kernels, on_device(): pl.pallas_call(kernel, out_shape=jax.ShapeDtypeStruct((16, 32, 128), F32)...  46.9 us
    unnamed x1, local copies, waits for them, and re-layouts  1.67 us

profile of v5, /device:TPU:1, one launch (start us, length us, event | category | flops | bytes accessed | tf_op | source)
XLA Modules:
  0.0 48.6 jit_solution(7487360805157807887)
XLA Ops:
  0.0 46.9 %shard_map.37 = f32[16,32,128]{2,1,0:T(8,128)} custom-call(f32[16,32,128]{2,1,0:T(8,128)} %g_hbm.1, f32[16,32,128]{2,1,0:T(8,128)} %c_hbm.1, f32[16,32,128]{2,1,0:T(8,128)} %v_hbm.1), custom_call_target="tpu_custom_call" | custom-call | tf_op jit(solution)/shard_map/pallas_call | solution.py:619
  46.9 1.7 %copy.5 = f32[16,32,128]{2,1,0:T(8,128)} copy(f32[16,32,128]{2,1,0:T(8,128)} %shard_map.37) | data formatting | bytes 524288

commit v6 on v5

--- a/solution.py
+++ b/solution.py
@@ -89,13 +89,13 @@
         RX=vm(5, 2, 32, 128), RY=vm(2, 5, 16, 1, 128), RZ=vm(2, 5, 32, 128), MZ=vm(5, 32, 128),
         ss=dma(42), rs=dma(42), W=vm(92, 8, 128), hs=dma(8), GV=vm(16, 32, 128), OV=vm(16, 32, 128),
     )
-    s.update(RS0=vm(8, 32, 128), RS1=vm(4, 24, 128), RS2=vm(8, 8, 128), QS=vm(4, 8, 128))
+    s.update(RS0=vm(8, 32, 128), RS1=vm(4, 24, 128), RS2=vm(8, 16, 128), QS=vm(4, 16, 128))
     for k, h in (("c", 5), ("g", 4)):
         s["B1" + k] = vm(8, 16, 128)
         s["PZ1" + k] = vm(16, 128)
         s["RX1" + k] = vm(2, h, 16, 128)
-        s["RY1" + k] = vm(2, 8, 8, 128)
-        s["RE1" + k] = vm(2, 2, h, 8, 128)
+        s["RY1" + k] = vm(2, 9, 8, 128)
+        s["RE1" + k] = vm(2, 2, h + 1, 8, 128)
         s["RZ1" + k] = vm(2, 3, 3, 16, 128)
         s["ZS" + k] = vm(3, 40, 128)
         s["PB2" + k] = vm(8, 128)
@@ -112,13 +112,13 @@
             s[name + l] = vm(16, 24, 128)
     s["wrap"] = pltpu.SemaphoreType.REGULAR((3,))
     s["K"] = pltpu.SMEM((2 * (CHEB - 1),), F32)
-    s.update(U2=vm(20, 24, 128), T21=vm(8, 24, 128), D21=vm(8, 24, 128))
+    s.update(U2=vm(20, 24, 128), T21=vm(8, 24, 128), D21=vm(8, 32, 128))
     s.update(TA=vm(10, 24, 128), TB=vm(10, 24, 128), DA=vm(10, 48, 128), DB=vm(10, 32, 128))
-    s.update(C3=vm(10, 48, 128), T3=vm(8, 32, 128), KA=vm(10, 48, 128), KB=vm(10, 48, 128), ST3=vm(8, 32, 128))
+    s.update(C3=vm(10, 48, 128), T3=vm(8, 40, 128), KA=vm(10, 48, 128), KB=vm(10, 48, 128), ST3=vm(8, 32, 128))
     s.update(WX3=vm(9, 32, 128), WY3=vm(8, 40, 128))
     for name in ("WXM3", "WXP3", "WYM3", "WYP3", "WZM3", "WZP3", "D3", "SD3"):
         s[name] = vm(8, 32, 128)
-    s.update(G3=vm(10, 8, 4, 128), R3=vm(8, 16, 128), T32=vm(8, 16, 128), D32=vm(8, 24, 128))
+    s.update(G3=vm(10, 8, 4, 128), R3=vm(8, 16, 128), T32=vm(8, 16, 128), D32=vm(8, 32, 128))
     return s
 
 
@@ -324,12 +324,12 @@
     def restrict_two(plane, k):
         rs, qs = s["RS2"], s["QS"]
         for q in range(8):
-            rs[q] = plane(2 * q) + plane(2 * q + 1)
+            rs[q, 0:8] = plane(2 * q) + plane(2 * q + 1)
         half = rs[:, pl.ds(0, 4, stride=2), :] + rs[:, pl.ds(1, 4, stride=2), :]
         for q in range(4):
             qs[q, 0:4] = half[2 * q]
             qs[q, 4:8] = half[2 * q + 1]
-        s["PB3" + k][...] = side_by_side(qs[...], to_three)
+        s["PB3" + k][...] = side_by_side(qs[:, 0:8, :], to_three)
 
     def send_one(k, h, axes=(0, 1)):
         out = []
@@ -341,11 +341,11 @@
                 xs = pl.ds(8 - h, h) if dx > 0 else pl.ds(0, h)
                 ys = pl.ds(8, 8) if dy > 0 else pl.ds(0, 8)
                 if dx and dy:
-                    src, dst = b.at[xs, ys], s["RE1" + k].at[side(-dx), side(-dy)]
+                    src, dst = b.at[xs, ys], s["RE1" + k].at[side(-dx), side(-dy), pl.ds(0, h)]
                 elif dx:
                     src, dst = b.at[xs], s["RX1" + k].at[side(-dx)]
                 else:
-                    src, dst = b.at[:, ys], s["RY1" + k].at[side(-dy)]
+                    src, dst = b.at[:, ys], s["RY1" + k].at[side(-dy), pl.ds(0, 8)]
             out.append(send(src, dst, ("one", k, (dx, dy) if axes else 0), (dx, dy, dz), axes))
         return grouped(out)
 
@@ -367,12 +367,12 @@
             planes = pl.ds(base, count)
             if dx == 0:
                 e[planes, 12:28, :] = b[...]
-                e[planes, 12 - h : 12, :] = keep(ry[0, :, 8 - h : 8, :], 0, -1, 0)
-                e[planes, 28 : 28 + h, :] = keep(ry[1, :, 0:h, :], 0, 1, 0)
+                e[planes, 12 - h : 12, :] = keep(ry[0, 0:8, 8 - h : 8, :], 0, -1, 0)
+                e[planes, 28 : 28 + h, :] = keep(ry[1, 0:8, 0:h, :], 0, 1, 0)
             else:
                 e[planes, 12:28, :] = keep(rx[side(dx)], dx, 0, 0)
-                e[planes, 12 - h : 12, :] = keep(re[side(dx), 0, :, 8 - h : 8, :], dx, -1, 0)
-                e[planes, 28 : 28 + h, :] = keep(re[side(dx), 1, :, 0:h, :], dx, 1, 0)
+                e[planes, 12 - h : 12, :] = keep(re[side(dx), 0, 0:h, 8 - h : 8, :], dx, -1, 0)
+                e[planes, 28 : 28 + h, :] = keep(re[side(dx), 1, 0:h, 0:h, :], dx, 1, 0)
             lo, hi = (8, 32) if h == 4 else (0, 40)
             at = lane((hi - lo, 128))
             halo = ((at >= 24) & (at < 32)) | ((at >= 96) & (at < 104))
@@ -529,8 +529,8 @@
     take_coarse(s["T3"], 0, 0, "g", g_chips)
     theta = constants()[1]
     for p in range(8):
-        t = s["T3"][p] * s["SD3"][p]
-        s["T3"][p] = t
+        t = s["T3"][p, 0:32, :] * s["SD3"][p]
+        s["T3"][p, 0:32, :] = t
         d = t * F32(1.0 / theta)
         s["ST3"][p] = d
         s["KA"][p + 1, 8:40, :] = d
@@ -540,7 +540,7 @@
         v = s[src]
         for p in range(8):
             e = v[p + 1, 8:40, :]
-            r = s["T3"][p] - e + s["WXM3"][p] * v[p, 8:40, :] + s["WXP3"][p] * v[p + 2, 8:40, :]
+            r = s["T3"][p, 0:32, :] - e + s["WXM3"][p] * v[p, 8:40, :] + s["WXP3"][p] * v[p + 2, 8:40, :]
             r = r + s["WYM3"][p] * v[p + 1, 7:39, :] + s["WYP3"][p] * v[p + 1, 9:41, :]
             r = r + s["WZM3"][p] * roll(e, 1) + s["WZP3"][p] * roll(e, -1)
             d = a * s["ST3"][p] + b * r
@@ -564,7 +564,7 @@
     for o in (0, 1):
         s["D32"][:, pl.ds(o, 12, stride=2), :] = s["T32"][:, 0:12, :]
     for p in range(16):
-        s["EA2"][p + 1, 8:32, :] = s["EB2"][p + 1, 8:32, :] + s["D32"][p // 2]
+        s["EA2"][p + 1, 8:32, :] = s["EB2"][p + 1, 8:32, :] + s["D32"][p // 2, 0:24, :]
     sweep("2", "EA2", "EB2")
     for p in range(16):
         right = s["G2"][p + 1, 8:32, :]
@@ -576,7 +576,7 @@
     for o in (0, 1):
         s["D21"][:, pl.ds(o, 12, stride=2), :] = s["T21"][:, 6:18, :]
     for p in range(1, 15):
-        s["EA1"][p + 1, 8:32, :] = s["EB1"][p + 1, 8:32, :] + s["D21"][p // 2]
+        s["EA1"][p + 1, 8:32, :] = s["EB1"][p + 1, 8:32, :] + s["D21"][p // 2, 0:24, :]
     sweep("1", "EA1", "EB1", range(2, 14))
     sweep("1", "EB1", "EA1", range(3, 13))
 

time: 48.7 us -> 48.7 us (level)
  no operation moved by 1% of the time
where the time goes in v6:
time: 48.7 us; the launch traced here: 48.6 us
  Pallas kernels  46.9 us (96%)
  local copies, waits for them, and re-layouts  1.67 us (3%)
    pallas_call x1, Pallas kernels, on_device(): pl.pallas_call(kernel, out_shape=jax.ShapeDtypeStruct((16, 32, 128), F32)...  46.9 us
    unnamed x1, local copies, waits for them, and re-layouts  1.67 us

profile of v6, /device:TPU:1, one launch (start us, length us, event | category | flops | bytes accessed | tf_op | source)
XLA Modules:
  0.0 48.6 jit_solution(15679526408052056544)
XLA Ops:
  0.0 46.9 %shard_map.37 = f32[16,32,128]{2,1,0:T(8,128)} custom-call(f32[16,32,128]{2,1,0:T(8,128)} %g_hbm.1, f32[16,32,128]{2,1,0:T(8,128)} %c_hbm.1, f32[16,32,128]{2,1,0:T(8,128)} %v_hbm.1), custom_call_target="tpu_custom_call" | custom-call | tf_op jit(solution)/shard_map/pallas_call | solution.py:619
  46.9 1.7 %copy.5 = f32[16,32,128]{2,1,0:T(8,128)} copy(f32[16,32,128]{2,1,0:T(8,128)} %shard_map.37) | data formatting | bytes 524288
